TPU v7x, 32 devices: a whole 2x2x4 slice. The times are simulated.
32 devices in a mesh: node: 4 (over y, x), feat: 8 (over z, core).
Axes of the slice: x: 2, y: 2, z: 4, core: 2. Of those that a mesh axis runs over, the one named last changes fastest.
Arguments:
- feats: bfloat16 [4096, 256], P(('node', 'feat')), may hold values from -6 to 6
- tile_values: bfloat16 [32, 24, 128, 128], P('node', 'feat'), may hold values from 0.049804688 to 1
- source_group: int32 [32, 24], P('node', 'feat'), may hold values from 0 to 3
- live_slots: int32 [32, 8], P('node', 'feat'), may hold values from 1 to 3, as said below
- proj_weight: bfloat16 [256, 256], replicated, may hold values from -0.375 to 0.375
- proj_bias: float32 [256], replicated, may hold values from -3 to 3
Outputs:
- updated: bfloat16 [4096, 256], P(('node', 'feat'))
Inputs may be any that keep to these rules, and one draw needn't show every extreme that they name: `live_slots`: some tile row has all 3 slots live in some column block; slots at or past the count are not part of A.
All inputs are finite; a program needn't handle non-finite values.
Results may differ from a plain program's by a relative error of at most 0.0028.
Values may be sent and summed in bfloat16 or wider, within the bound.
No kernel may reach another device: no remote copies, remote signals or barrier semaphores. Data moves between devices by JAX's collectives and lax.ppermute only.
A program may use at most 64 MiB of HBM per device.

v0:
```python
import math

import jax
import jax.numpy as jnp
from jax import lax
from jax.sharding import PartitionSpec as P


def degrees(tiles, live_count):
    slot_index = jnp.arange(tiles.shape[1], dtype=jnp.int32)
    keep_slot = slot_index[None, :] < live_count
    per_row = jnp.sum(tiles, axis=3, dtype=jnp.float32)
    per_row = jnp.where(keep_slot[:, :, None], per_row, jnp.zeros_like(per_row))
    return jnp.sum(per_row, axis=1).reshape(-1)


def aggregate_rows(tiles, sources, live_count, source_rows):
    tile_size = source_rows.shape[1]
    width = source_rows.shape[2]
    row_count = tiles.shape[0]
    block_rows = math.gcd(row_count, 8)
    block_count = row_count // block_rows
    slot_index = jnp.arange(tiles.shape[1], dtype=jnp.int32)

    def one_block(block_args):
        block_tiles, block_sources, block_live = block_args
        keep_slot = slot_index[None, :] < block_live
        adjacency = jnp.where(keep_slot[:, :, None, None], block_tiles, jnp.zeros_like(block_tiles))
        gathered = jnp.take(source_rows, block_sources, axis=0)
        return jnp.einsum("rsab,rsbf->raf", adjacency, gathered, preferred_element_type=jnp.float32)

    block_args = (
        tiles.reshape((block_count, block_rows) + tiles.shape[1:]),
        sources.reshape(block_count, block_rows, -1),
        live_count.reshape(block_count, block_rows, -1),
    )
    products = lax.map(one_block, block_args)
    return products.reshape(row_count * tile_size, width)


def body(feats, tile_values, source_group, live_slots, proj_weight, proj_bias):
    tile_size = feats.shape[0]
    width = feats.shape[1]
    gathered = lax.all_gather(feats, "node", axis=0, tiled=True)
    source_rows = gathered.reshape(-1, tile_size, width)
    partials = aggregate_rows(tile_values, source_group, live_slots, source_rows)
    aggregate, degree_sum = (
        lax.psum_scatter(partials, "feat", scatter_dimension=0, tiled=True),
        lax.psum_scatter(degrees(tile_values, live_slots), "feat", scatter_dimension=0, tiled=True),
    )
    own_rows = feats.astype(jnp.float32)
    inv_root = lax.rsqrt(degree_sum + 1.0)
    normed = ((aggregate + own_rows) * inv_root[:, None]).astype(jnp.bfloat16)
    hidden = jnp.dot(normed, proj_weight, preferred_element_type=jnp.float32) + proj_bias
    return (own_rows + jax.nn.relu(hidden)).astype(jnp.bfloat16)


def solution(mesh):
    placed = (
        P(("node", "feat"), None),
        P("node", "feat", None, None),
        P("node", "feat"),
        P("node", "feat"),
        P(),
        P(),
    )
    return jax.shard_map(
        body, mesh=mesh, in_specs=placed, out_specs=P(("node", "feat"), None), check_vma=False
    )
```

profile of v0, /device:TPU:0, one launch (start us, length us, event | category | flops | bytes accessed | tf_op | source)
XLA Modules:
  0.0 64.0 jit_solution(16480867638635272305)
XLA Ops:
  6.5 0.0 copy-start
  6.5 0.0 reduce-scatter.2.cloned.1.call-start
  6.5 0.7 %compare_select_fusion = s32[8,3]{0,1:T(4,128)S(1)} fusion(s32[8,3]{0,1:T(4,128)} %param.8), kind=kLoop, calls=%fused_computation.18 | loop fusion | flops 72 | bytes 192 | tf_op jit(solution)/shard_map/while/body/eval_jaxpr/jit(_take)/jit(_where)/select_n | solution.py:29
  7.3 0.7 %compare_and_fusion = pred[8,3]{0,1:T(4,128)(4,1)S(1)} fusion(s32[8,3]{0,1:T(4,128)} %param.8), kind=kLoop, calls=%fused_computation.21 | loop fusion | flops 144 | bytes 120 | tf_op jit(solution)/shard_map/while/body/eval_jaxpr/jit(_take)/and | solution.py:29
  7.9 0.7 %iota_compare_fusion = pred[8,3]{1,0:T(8,128)(4,1)S(1)} fusion(s32[8]{0:T(128)} %bitcast.14), kind=kLoop, calls=%fused_computation.20 | loop fusion | flops 24 | bytes 56 | tf_op jit(solution)/shard_map/while/body/eval_jaxpr/lt | solution.py:27
  8.7 10.7 %all_gather.3 = bf16[512,256]{1,0:T(8,128)(2,1)S(1)} all-gather(bf16[128,256]{1,0:T(8,128)(2,1)} %param.6), channel_id=1, replica_groups=mesh['node'=4,'feat'=8] {'node'}, dimensions={0}, use_global_device_ids=true | all-gather | bytes 327680 | tf_op jit(solution)/shard_map/all_gather | solution.py:44
  19.4 0.1 copy.17
  19.5 0.1 reshape.75
  19.6 0.1 copy.16
  19.7 0.0 copy-start.1
  19.7 0.7 %gather_fusion = bf16[24,128,256]{2,1,0:T(8,128)(2,1)S(1)} fusion(bf16[4,128,256]{2,1,0:T(8,128)(2,1)S(1)} %bitcast.10, s32[1024]{0:T(1024)S(1)} %pad_clamp_fusion), kind=kCustom, calls=%fused_computation | custom fusion | bytes 3145824 | tf_op jit(solution)/shard_map/while/body/eval_jaxpr/jit(_take)/gather | solution.py:29
  20.3 0.5 copy-done.1
  20.8 0.0 copy-start.4
  20.8 1.5 %fusion = f32[8,128,256,1]{2,1,3,0:T(8,128)} fusion(bf16[8,3,128,256]{3,2,1,0:T(8,128)(2,1)S(1)} %bitcast.11, pred[8,3]{1,0:T(8,128)(4,1)S(1)} %copy.16, bf16[8,3,128,128]{3,2,1,0:T(8,128)(2,1)S(1)} %copy-done.1, pred[8,3]{1,0:T(8,128)(4,1)S(1)} %iota_compare_fusion), kind=kOutput, calls=%fused_computation.2 | convolution fusion | flops 202506240 | bytes 3407920 | tf_op jit(solution)/shard_map/while/body/eval_jaxpr/rsab,rsbf->raf/dot_general | solution.py:30
  22.3 0.0 copy-start.2
  22.3 0.0 copy-start.3
  22.3 0.0 reduce-scatter.2.cloned.1.call-update
  22.3 0.0 copy-done.4
  22.4 0.6 dynamic-slice.3
  23.6 0.3 convert_reduce_fusion
  23.9 0.1 select_reduce_fusion
  24.0 15.0 %all-reduce = f32[1024]{0:T(1024)S(1)} all-reduce(f32[1024]{0:T(1024)S(1)} %bitcast.13), channel_id=3, replica_groups=mesh['node'=4,'feat'=8] {'feat'}, use_global_device_ids=true, to_apply=%region_3.4.clone | all-reduce | flops 1024 | bytes 8192
  39.0 0.1 fusion.14
  39.1 16.3 %reduce-scatter.2.cloned.1.call-done = f32[128,256]{1,0:T(8,128)} async-done(((f32[1024,256]{1,0:T(8,128)}), f32[128,256]{1,0:T(8,128)}) %reduce-scatter.2.cloned.1.call-update) | async-done | bytes 131088 | tf_op jit(solution)/shard_map/reduce_scatter | solution.py:48
  55.4 0.0 copy-done
  55.4 0.0 copy-done.2
  55.4 0.0 copy-done.3
  55.4 1.8 %fusion.5 = bf16[128,256]{1,0:T(8,128)(2,1)} fusion(bf16[256,256]{1,0:T(8,128)(2,1)S(1)} %copy-done, bf16[128,256]{1,0:T(8,128)(2,1)S(1)} %copy-done.2, f32[128,256]{1,0:T(8,128)} %reduce-scatter.2.cloned.1.call-done, f32[256]{0:T(256)S(1)} %copy-done.3, f32[128]{0:T(128)S(1)} %fusion.14), kind=kOutput, calls=%fused_computation.8 | convolution fusion | flops 17072128 | bytes 394752 | tf_op jit(solution)/shard_map/dot_general | solution.py:54
  (1 shorter events, 0.0 us)
Async XLA Ops:
  6.5 48.8 %copy-start = (bf16[256,256]{1,0:T(8,128)(2,1)S(1)}, bf16[256,256]{1,0:T(8,128)(2,1)}, u32[]{:S(2)}) copy-start(bf16[256,256]{1,0:T(8,128)(2,1)} %param.10) | copy-start | bytes 393220
  6.5 48.8 %reduce-scatter.2.cloned.1.call-start = ((), (), s32[]{:S(2)}) async-start(), calls=%async_computation.1 | async-start | bytes 1179648 | tf_op jit(solution)/shard_map/reduce_scatter | solution.py:48
  19.7 1.1 %copy-start.1 = (bf16[8,3,128,128]{3,2,1,0:T(8,128)(2,1)S(1)}, bf16[8,3,128,128]{3,2,1,0:T(8,128)(2,1)}, u32[]{:S(2)}) copy-start(bf16[8,3,128,128]{3,2,1,0:T(8,128)(2,1)} %param.7) | copy-start | bytes 2359300
  20.8 1.6 %copy-start.4 = (u32[32]{0:T(128)S(1)}, u32[32]{0:T(128)}, u32[]{:S(2)}) copy-start(u32[32]{0:T(128)} %constant.49) | copy-start | bytes 388
  22.3 33.1 %copy-start.2 = (bf16[128,256]{1,0:T(8,128)(2,1)S(1)}, bf16[128,256]{1,0:T(8,128)(2,1)}, u32[]{:S(2)}) copy-start(bf16[128,256]{1,0:T(8,128)(2,1)} %param.6) | copy-start | bytes 196612
  22.3 33.1 %copy-start.3 = (f32[256]{0:T(256)S(1)}, f32[256]{0:T(256)}, u32[]{:S(2)}) copy-start(f32[256]{0:T(256)} %param.11) | copy-start | bytes 3076
Sparse Core Ops, SparseCore 0:
  22.5 32.8 reduce-scatter.1
where the time goes:
time: 64.3 us; the launch traced here: 64 us
  blocking collectives  25.7 us (40%)
  waiting for transfers between devices  16.3 us (25%)
  between operations  14.1 us (22%)
  matrix products  3.27 us (5%)
  other arithmetic  2.6 us (4%)
  local copies, waits for them, and re-layouts  1.99 us (3%)
    reduce_scatter x1, waiting for transfers between devices, body(): lax.psum_scatter(partials, 'feat', scatter_dimension=0, tiled=True)  16.3 us
    unnamed x1, blocking collectives  15 us
    all_gather x1, blocking collectives, body(): gathered = lax.all_gather(feats, 'node', axis=0, tiled=True)  10.7 us
    dot_general x1, matrix products, body(): jnp.dot(normed, proj_weight, preferred_element_type=jnp.float32) + proj_bias  1.75 us
    dot_general x1, matrix products, one_block(): jnp.einsum('rsab,rsbf->raf', adjacency, gathered, preferred_element_type=...  1.52 us
  transfers between devices with their start and end apart: 1, of which 1 were waited for; matrix products, arithmetic and copies ran while one was open for 2% of the time, Pallas kernels for 0%

commit v1 on v0

v1 whole, which is shorter than its diff:
```python
import functools

import jax
import jax.numpy as jnp
from jax import lax
from jax.experimental import pallas as pl
from jax.experimental.pallas import tpu as pltpu
from jax.sharding import PartitionSpec as P

EXTRA = 16
VMEM = pl.BlockSpec(memory_space=pltpu.VMEM)
SMEM = pl.BlockSpec(memory_space=pltpu.SMEM)
ANY = pl.BlockSpec(memory_space=pl.ANY)
PARAMS = pltpu.CompilerParams(vmem_limit_bytes=32 * 1024 * 1024)


def partner(index, step, count):
    if count & (count - 1) == 0:
        return index ^ step
    return (index + step) % count


def partner_back(index, step, count):
    if count & (count - 1) == 0:
        return index ^ step
    return (index + count - step) % count


def split_rows(degree):
    high = degree.astype(jnp.bfloat16)
    low = (degree - high.astype(jnp.float32)).astype(jnp.bfloat16)
    return jnp.concatenate([high, low], axis=1)


def join_rows(rows):
    rows = rows.astype(jnp.float32)
    half = rows.shape[1] // 2
    return rows[:, :half] + rows[:, half:]


def prepare_kernel(live, tiles, adjacency, degree):
    groups, slots, tile, _ = tiles.shape
    ones = jnp.ones((EXTRA, slots * tile), jnp.bfloat16)
    for group in range(groups):
        count = live[group, 0]
        wide = []
        for slot in range(slots):
            block = tiles[group, slot]
            wide.append(jnp.where(slot < count, block, jnp.zeros_like(block)))
        wide = jnp.concatenate(wide, axis=1)
        adjacency[group] = wide
        degree[group] = lax.dot_general(
            ones, wide, (((1,), (1,)), ((), ())), preferred_element_type=jnp.float32
        )


def aggregate_kernel(nodes, chips, slots, mine, *refs):
    src, adjacency, degree = refs[:3]
    feats_in = refs[3 : 3 + nodes]
    out, rows = refs[3 + nodes :]
    node = lax.axis_index("node")
    feat = lax.axis_index("feat")
    chip = feat // 2
    core = feat % 2 if mine else 1 - feat % 2
    tile = feats_in[0].shape[0]
    for step in range(nodes):
        rows[partner_back(node, step, nodes)] = feats_in[step][...]
    for step in range(chips):
        group = partner(chip, step, chips) * 2 + core
        right = jnp.concatenate([rows[src[group, slot]] for slot in range(slots)], axis=0)
        product = jnp.dot(adjacency[group], right, preferred_element_type=jnp.float32)
        out[step, :tile] = product.astype(out.dtype)
        out[step, tile:] = split_rows(degree[group]).astype(out.dtype)


def merge_kernel(mine, theirs, own, *outs):
    tile = mine.shape[1] - EXTRA
    for step in range(mine.shape[0]):
        total = mine[step, :tile] + theirs[step, :tile].astype(jnp.float32)
        degree = split_rows(join_rows(mine[step, tile:]) + join_rows(theirs[step, tile:]))
        out = outs[step - 1] if step else own
        out[:tile] = total.astype(out.dtype)
        out[tile:] = degree.astype(out.dtype)


def update_kernel(*refs):
    own, *parts, feats, weight, bias, out = refs
    tile = feats.shape[0]
    total = own[...]
    for part in parts:
        total = total + part[...].astype(jnp.float32)
    degree = join_rows(total[tile:])[:1]
    scale = jnp.transpose(jnp.broadcast_to(lax.rsqrt(degree + 1.0), (tile, tile)))
    scale = jnp.concatenate([scale] * (feats.shape[1] // tile), axis=1)
    rows = feats[...].astype(jnp.float32)
    normed = ((total[:tile] + rows) * scale).astype(jnp.bfloat16)
    hidden = jnp.dot(normed, weight[...], preferred_element_type=jnp.float32) + bias[...]
    out[...] = (rows + jnp.maximum(hidden, 0.0)).astype(jnp.bfloat16)


def body(mesh, feats, tile_values, source_group, live_slots, proj_weight, proj_bias):
    nodes, chips = mesh.shape["node"], mesh.shape["feat"] // 2
    groups, slots = tile_values.shape[:2]
    tile, width = feats.shape

    def over_nodes(step):
        pairs = [(n, partner(n, step, nodes)) for n in range(nodes)]
        return lax.ppermute(feats, "node", pairs)

    def over_chips(array, step):
        pairs = [(2 * z + c, 2 * partner(z, step, chips) + c) for z in range(chips) for c in range(2)]
        return lax.ppermute(array, "feat", pairs)

    def over_cores(array):
        return lax.ppermute(array, "feat", [(f, f ^ 1) for f in range(2 * chips)])

    rows_in = [feats] + [over_nodes(step) for step in range(1, nodes)]
    adjacency, degree = pl.pallas_call(
        prepare_kernel,
        out_shape=[
            jax.ShapeDtypeStruct((groups, tile, slots * tile), jnp.bfloat16),
            jax.ShapeDtypeStruct((groups, EXTRA, tile), jnp.float32),
        ],
        in_specs=[SMEM, VMEM],
        out_specs=[VMEM, VMEM],
        compiler_params=PARAMS,
        cost_estimate=pl.CostEstimate(flops=1 << 27, bytes_accessed=1 << 22, transcendentals=0),
    )(live_slots, tile_values)

    def aggregate(mine):
        dtype = jnp.float32 if mine else jnp.bfloat16
        return pl.pallas_call(
            functools.partial(aggregate_kernel, nodes, chips, slots, mine),
            out_shape=jax.ShapeDtypeStruct((chips, tile + EXTRA, width), dtype),
            in_specs=[SMEM] + [VMEM] * (2 + nodes),
            out_specs=VMEM,
            scratch_shapes=[pltpu.VMEM((nodes, tile, width), jnp.bfloat16)],
            compiler_params=PARAMS,
            cost_estimate=pl.CostEstimate(flops=1 << 27, bytes_accessed=1 << 22, transcendentals=0),
        )(source_group, adjacency, degree, *rows_in)

    theirs = over_cores(aggregate(False))
    own, *parts = pl.pallas_call(
        merge_kernel,
        out_shape=[jax.ShapeDtypeStruct((tile + EXTRA, width), jnp.float32)]
        + [jax.ShapeDtypeStruct((tile + EXTRA, width), jnp.bfloat16)] * (chips - 1),
        in_specs=[VMEM] * 2,
        out_specs=[VMEM] * chips,
        compiler_params=PARAMS,
    )(aggregate(True), theirs)
    parts = [over_chips(part, step) for step, part in enumerate(parts, 1)]
    return pl.pallas_call(
        update_kernel,
        out_shape=jax.ShapeDtypeStruct((tile, width), jnp.bfloat16),
        in_specs=[VMEM] * (chips + 3),
        out_specs=VMEM,
        compiler_params=PARAMS,
    )(own, *parts, feats, proj_weight, proj_bias.reshape(1, -1))


def solution(mesh):
    placed = (
        P(("node", "feat"), None),
        P("node", "feat", None, None),
        P("node", "feat"),
        P("node", "feat"),
        P(),
        P(),
    )
    return jax.shard_map(
        functools.partial(body, mesh),
        mesh=mesh,
        in_specs=placed,
        out_specs=P(("node", "feat"), None),
        check_vma=False,
    )
```

time: 64.3 us -> 23.8 us (0.37)
  blocking collectives: 25.7 us -> 0 us
  between operations: 14.1 us -> 0.05 us
  starting transfers between devices: 0.01 us -> 9.04 us
  waiting for transfers between devices: 16.3 us -> 8.04 us
  Pallas kernels: 0 us -> 3.82 us
  matrix products: 3.27 us -> 0 us
  other arithmetic: 2.6 us -> 0 us
  local copies, waits for them, and re-layouts: 1.99 us -> 2.66 us
    reduce_scatter x1 -> x0, waiting for transfers between devices: 16.3 us -> none  [body(): lax.psum_scatter(partials, 'feat', scatter_dimension=0, tiled=True)]
    unnamed x1 -> x0, blocking collectives: 15 us -> none
    all_gather x1 -> x0, blocking collectives: 10.7 us -> none  [body(): gathered = lax.all_gather(feats, 'node', axis=0, tiled=True)]
    ppermute x0 -> x7, starting transfers between devices: none -> 9.04 us  [the longest x3 4.52 us: over_nodes(): return lax.ppermute(feats, 'node', pairs)]
    ppermute x0 -> x7, waiting for transfers between devices: none -> 8.04 us  [the longest x3 6.05 us: over_chips(): return lax.ppermute(array, 'feat', pairs)]
    pallas_call x0 -> x5, Pallas kernels: none -> 3.82 us  [the longest x2 1.88 us: aggregate(): pl.pallas_call(functools.partial(aggregate_kernel, nodes, chips, slots, m...]
    dot_general x2 -> x0, matrix products: 3.27 us -> none  [the longest x1 1.75 us: body(): jnp.dot(normed, proj_weight, preferred_element_type=jnp.float32) + proj_bias]
    unnamed x11 -> x12, local copies, waits for them, and re-layouts: 1.08 us -> 2.66 us
  transfers between devices with their start and end apart: 1 -> 7, of which waited for: 1 -> 4; matrix products, arithmetic and copies ran while one was open for 2% -> 4% of each run, Pallas kernels for 0% -> 8%
where the time goes in v1:
time: 23.8 us; the launch traced here: 23.6 us
  starting transfers between devices  9.04 us (38%)
  waiting for transfers between devices  8.04 us (34%)
  Pallas kernels  3.82 us (16%)
  local copies, waits for them, and re-layouts  2.66 us (11%)
    ppermute x3, waiting for transfers between devices, over_chips(): return lax.ppermute(array, 'feat', pairs)  6.05 us
    ppermute x3, starting transfers between devices, over_nodes(): return lax.ppermute(feats, 'node', pairs)  4.52 us
    ppermute x3, starting transfers between devices, over_chips(): return lax.ppermute(array, 'feat', pairs)  4.45 us
    unnamed x12, local copies, waits for them, and re-layouts  2.66 us
    pallas_call x2, Pallas kernels, aggregate(): pl.pallas_call(functools.partial(aggregate_kernel, nodes, chips, slots, m...  1.88 us
    ppermute x3, waiting for transfers between devices, over_nodes(): return lax.ppermute(feats, 'node', pairs)  1.38 us
    pallas_call x1, Pallas kernels, body(): pl.pallas_call(prepare_kernel, out_shape=[jax.ShapeDtypeStruct((groups, t...  1 us
    pallas_call x1, Pallas kernels, body(): pl.pallas_call(update_kernel, out_shape=jax.ShapeDtypeStruct((tile, width...  0.87 us
  transfers between devices with their start and end apart: 7, of which 4 were waited for; matrix products, arithmetic and copies ran while one was open for 4% of the time, Pallas kernels for 8%

profile of v1, /device:TPU:0, one launch (start us, length us, event | category | flops | bytes accessed | tf_op | source)
XLA Modules:
  0.0 23.6 jit_solution(2920843514563460664)
XLA Ops:
  0.0 0.0 copy-start.4
  0.0 3.9 %collective-permute-start.2 = (bf16[128,256]{1,0:T(8,128)(2,1)}, bf16[128,256]{1,0:T(8,128)(2,1)S(1)}, u32[]{:S(2)}, u32[]{:S(2)}) collective-permute-start(bf16[128,256]{1,0:T(8,128)(2,1)} %refs_4_.1), channel_id=1, source_target_pairs={{0,24},{8,16},{16,8},{24,0},{1,25},{9,17},{17,9},{25,1},{2,26},{10... | collective-permute-start | bytes 196616 | tf_op jit(solution)/shard_map/ppermute | solution.py:108
  3.9 0.5 %collective-permute-start.1 = (bf16[128,256]{1,0:T(8,128)(2,1)}, bf16[128,256]{1,0:T(8,128)(2,1)S(1)}, u32[]{:S(2)}, u32[]{:S(2)}) collective-permute-start(bf16[128,256]{1,0:T(8,128)(2,1)} %refs_4_.1), channel_id=1, source_target_pairs={{0,16},{8,24},{16,0},{24,8},{1,17},{9,25},{17,1},{25,9},{2,18},{10... | collective-permute-start | bytes 196616 | tf_op jit(solution)/shard_map/ppermute | solution.py:108
  4.4 0.1 collective-permute-start
  4.5 0.8 %copy.8.refs_0_ = s32[8,3]{1,0:T(8,128)S(1)} copy(s32[8,3]{0,1:T(4,128)} %param.8) | data formatting | bytes 192 | tf_op args[2]
  5.3 0.0 copy-done.4
  5.3 0.1 copy.7.live
  5.4 0.0 copy-start
  5.4 1.1 %copy-done = bf16[8,3,128,128]{3,2,1,0:T(8,128)(2,1)S(1)} copy-done((bf16[8,3,128,128]{3,2,1,0:T(8,128)(2,1)S(1)}, bf16[8,3,128,128]{3,2,1,0:T(8,128)(2,1)}, u32[]{:S(2)}) %copy-start) | copy-done | bytes 786456
  6.5 0.0 copy-start.1
  6.5 1.0 %shard_map.64 = (bf16[8,128,384]{2,1,0:T(8,128)(2,1)S(1)}, f32[8,16,128]{2,1,0:T(8,128)S(1)}) custom-call(s32[8,1]{1,0:T(8,128)S(1)} %copy.7.live, bf16[8,3,128,128]{3,2,1,0:T(8,128)(2,1)S(1)} %copy-done), custom_call_target="tpu_custom_call" | custom-call | flops 134217728 | bytes 4194304 | tf_op jit(solution)/shard_map/pallas_call | solution.py:118
  7.5 0.0 collective-permute-done.2.refs_6_
  7.5 0.9 %collective-permute-done.1.refs_5_ = bf16[128,256]{1,0:T(8,128)(2,1)S(1)} collective-permute-done((bf16[128,256]{1,0:T(8,128)(2,1)}, bf16[128,256]{1,0:T(8,128)(2,1)S(1)}, u32[]{:S(2)}, u32[]{:S(2)}) %collective-permute-start.1) | collective-permute-done | bytes 65568 | tf_op jit(solution)/shard_map/ppermute | solution.py:108
  8.4 0.5 %collective-permute-done.refs_4_ = bf16[128,256]{1,0:T(8,128)(2,1)S(1)} collective-permute-done((bf16[128,256]{1,0:T(8,128)(2,1)}, bf16[128,256]{1,0:T(8,128)(2,1)S(1)}, u32[]{:S(2)}, u32[]{:S(2)}) %collective-permute-start) | collective-permute-done | bytes 65568 | tf_op jit(solution)/shard_map/ppermute | solution.py:108
  8.9 0.0 copy-done.1
  8.9 0.9 %shard_map.66 = bf16[4,144,256]{2,1,0:T(8,128)(2,1)S(1)} custom-call(s32[8,3]{1,0:T(8,128)S(1)} %copy.8.refs_0_, bf16[8,128,384]{2,1,0:T(8,128)(2,1)S(1)} %get-tuple-element.11.refs_1_, f32[8,16,128]{2,1,0:T(8,128)S(1)} %get-tuple-element.12.refs_2_, bf16[128,256]{1,0:T(8,128)(2,1)S(1)} %copy-done.1, bf16[128,256]{1,0:T(8,128)(2,1)S(1)} %collective-permute-done.refs_4_, ...), custom_call_target="tpu_custom_call" | custom-call | flops 134217728 | bytes 4194304 | tf_op jit(solution)/shard_map/pallas_call | solution.py:132
  9.8 0.1 collective-permute-start.3
  9.9 0.9 %shard_map.65.mine = f32[4,144,256]{2,1,0:T(8,128)S(1)} custom-call(s32[8,3]{1,0:T(8,128)S(1)} %copy.8.refs_0_, bf16[8,128,384]{2,1,0:T(8,128)(2,1)S(1)} %get-tuple-element.11.refs_1_, f32[8,16,128]{2,1,0:T(8,128)S(1)} %get-tuple-element.12.refs_2_, bf16[128,256]{1,0:T(8,128)(2,1)S(1)} %copy-done.1, bf16[128,256]{1,0:T(8,128)(2,1)S(1)} %collective-permute-done.refs_4_, ...), custom_call_target="tpu_custom_call" | custom-call | flops 134217728 | bytes 4194304 | tf_op jit(solution)/shard_map/pallas_call | solution.py:132
  10.9 0.0 copy-start.2
  10.9 0.6 %collective-permute-done.3.theirs = bf16[4,144,256]{2,1,0:T(8,128)(2,1)S(1)} collective-permute-done((bf16[4,144,256]{2,1,0:T(8,128)(2,1)S(1)}, bf16[4,144,256]{2,1,0:T(8,128)(2,1)S(1)}, u32[]{:S(2)}, u32[]{:S(2)}) %collective-permute-start.3) | collective-permute-done | bytes 294944 | tf_op jit(solution)/shard_map/ppermute | solution.py:115
  11.5 0.1 shard_map.67
  11.6 1.6 %collective-permute-start.4 = (bf16[144,256]{1,0:T(8,128)(2,1)S(1)}, bf16[144,256]{1,0:T(8,128)(2,1)S(1)}, u32[]{:S(2)}, u32[]{:S(2)}) collective-permute-start(bf16[144,256]{1,0:T(8,128)(2,1)S(1)} %get-tuple-element.14), channel_id=1, source_target_pairs={{0,2},{1,3},{2,0},{3,1},{4,6},{5,7},{6,4},{7,5},{8,10},{9,11},{10,... | collective-permute-start | bytes 221192 | tf_op jit(solution)/shard_map/ppermute | solution.py:112
  13.2 2.6 %collective-permute-start.5 = (bf16[144,256]{1,0:T(8,128)(2,1)S(1)}, bf16[144,256]{1,0:T(8,128)(2,1)S(1)}, u32[]{:S(2)}, u32[]{:S(2)}) collective-permute-start(bf16[144,256]{1,0:T(8,128)(2,1)S(1)} %get-tuple-element.15), channel_id=1, source_target_pairs={{0,4},{1,5},{2,6},{3,7},{4,0},{5,1},{6,2},{7,3},{8,12},{9,13},{10,... | collective-permute-start | bytes 221192 | tf_op jit(solution)/shard_map/ppermute | solution.py:112
  15.8 0.2 collective-permute-start.6
  16.0 0.0 collective-permute-done.4.refs_1_
  16.0 6.0 %collective-permute-done.5.refs_2_ = bf16[144,256]{1,0:T(8,128)(2,1)S(1)} collective-permute-done((bf16[144,256]{1,0:T(8,128)(2,1)S(1)}, bf16[144,256]{1,0:T(8,128)(2,1)S(1)}, u32[]{:S(2)}, u32[]{:S(2)}) %collective-permute-start.5) | collective-permute-done | bytes 73760 | tf_op jit(solution)/shard_map/ppermute | solution.py:112
  22.1 0.0 collective-permute-done.6.refs_3_
  22.1 0.0 copy-start.3
  22.1 0.0 copy-done.2
  22.1 0.7 %copy-done.3 = f32[256]{0:T(256)S(1)} copy-done((f32[256]{0:T(256)S(1)}, f32[256]{0:T(256)}, u32[]{:S(2)}) %copy-start.3) | copy-done | bytes 1048
  22.7 0.9 %shard_map.68 = bf16[128,256]{1,0:T(8,128)(2,1)} custom-call(f32[144,256]{1,0:T(8,128)S(1)} %get-tuple-element.13.refs_0_, bf16[144,256]{1,0:T(8,128)(2,1)S(1)} %collective-permute-done.4.refs_1_, bf16[144,256]{1,0:T(8,128)(2,1)S(1)} %collective-permute-done.5.refs_2_, bf16[144,256]{1,0:T(8,128)(2,1)S(1)} %collective-permute-done.6.refs_3_, ...), custom_call_target="tpu_custom_call" | custom-call | tf_op jit(solution)/shard_map/pallas_call | solution.py:152
Async XLA Ops:
  0.0 5.3 %copy-start.4 = (s32[8,1]{0,1:T(1,128)S(1)}, s32[8,1]{0,1:T(1,128)}, u32[]{:S(2)}) copy-start(s32[8,1]{0,1:T(1,128)} %param.9) | copy-start | bytes 100
  0.0 7.5 %collective-permute-start.2 = (bf16[128,256]{1,0:T(8,128)(2,1)}, bf16[128,256]{1,0:T(8,128)(2,1)S(1)}, u32[]{:S(2)}, u32[]{:S(2)}) collective-permute-start(bf16[128,256]{1,0:T(8,128)(2,1)} %refs_4_.1), channel_id=1, source_target_pairs={{0,24},{8,16},{16,8},{24,0},{1,25},{9,17},{17,9},{25,1},{2,26},{10... | collective-permute-start | bytes 196616 | tf_op jit(solution)/shard_map/ppermute | solution.py:108
  3.9 4.5 %collective-permute-start.1 = (bf16[128,256]{1,0:T(8,128)(2,1)}, bf16[128,256]{1,0:T(8,128)(2,1)S(1)}, u32[]{:S(2)}, u32[]{:S(2)}) collective-permute-start(bf16[128,256]{1,0:T(8,128)(2,1)} %refs_4_.1), channel_id=1, source_target_pairs={{0,16},{8,24},{16,0},{24,8},{1,17},{9,25},{17,1},{25,9},{2,18},{10... | collective-permute-start | bytes 196616 | tf_op jit(solution)/shard_map/ppermute | solution.py:108
  4.4 4.5 %collective-permute-start = (bf16[128,256]{1,0:T(8,128)(2,1)}, bf16[128,256]{1,0:T(8,128)(2,1)S(1)}, u32[]{:S(2)}, u32[]{:S(2)}) collective-permute-start(bf16[128,256]{1,0:T(8,128)(2,1)} %refs_4_.1), channel_id=1, source_target_pairs={{0,8},{8,0},{16,24},{24,16},{1,9},{9,1},{17,25},{25,17},{2,10},{10... | collective-permute-start | bytes 196616 | tf_op jit(solution)/shard_map/ppermute | solution.py:108
  5.4 1.1 %copy-start = (bf16[8,3,128,128]{3,2,1,0:T(8,128)(2,1)S(1)}, bf16[8,3,128,128]{3,2,1,0:T(8,128)(2,1)}, u32[]{:S(2)}) copy-start(bf16[8,3,128,128]{3,2,1,0:T(8,128)(2,1)} %tiles.1) | copy-start | bytes 2359300
  6.5 2.4 %copy-start.1 = (bf16[128,256]{1,0:T(8,128)(2,1)S(1)}, bf16[128,256]{1,0:T(8,128)(2,1)}, u32[]{:S(2)}) copy-start(bf16[128,256]{1,0:T(8,128)(2,1)} %refs_4_.1) | copy-start | bytes 196612
  9.8 1.6 %collective-permute-start.3 = (bf16[4,144,256]{2,1,0:T(8,128)(2,1)S(1)}, bf16[4,144,256]{2,1,0:T(8,128)(2,1)S(1)}, u32[]{:S(2)}, u32[]{:S(2)}) collective-permute-start(bf16[4,144,256]{2,1,0:T(8,128)(2,1)S(1)} %shard_map.66), channel_id=1, source_target_pairs={{0,1},{1,0},{2,3},{3,2},{4,5},{5,4},{6,7},{7,6},{8,9},{9,8},{10,11... | collective-permute-start | bytes 884744 | tf_op jit(solution)/shard_map/ppermute | solution.py:115
  10.9 11.2 %copy-start.2 = (bf16[256,256]{1,0:T(8,128)(2,1)S(1)}, bf16[256,256]{1,0:T(8,128)(2,1)}, u32[]{:S(2)}) copy-start(bf16[256,256]{1,0:T(8,128)(2,1)} %refs_5_.1) | copy-start | bytes 393220
  11.6 4.5 %collective-permute-start.4 = (bf16[144,256]{1,0:T(8,128)(2,1)S(1)}, bf16[144,256]{1,0:T(8,128)(2,1)S(1)}, u32[]{:S(2)}, u32[]{:S(2)}) collective-permute-start(bf16[144,256]{1,0:T(8,128)(2,1)S(1)} %get-tuple-element.14), channel_id=1, source_target_pairs={{0,2},{1,3},{2,0},{3,1},{4,6},{5,7},{6,4},{7,5},{8,10},{9,11},{10,... | collective-permute-start | bytes 221192 | tf_op jit(solution)/shard_map/ppermute | solution.py:112
  13.2 8.9 %collective-permute-start.5 = (bf16[144,256]{1,0:T(8,128)(2,1)S(1)}, bf16[144,256]{1,0:T(8,128)(2,1)S(1)}, u32[]{:S(2)}, u32[]{:S(2)}) collective-permute-start(bf16[144,256]{1,0:T(8,128)(2,1)S(1)} %get-tuple-element.15), channel_id=1, source_target_pairs={{0,4},{1,5},{2,6},{3,7},{4,0},{5,1},{6,2},{7,3},{8,12},{9,13},{10,... | collective-permute-start | bytes 221192 | tf_op jit(solution)/shard_map/ppermute | solution.py:112
  15.8 6.3 %collective-permute-start.6 = (bf16[144,256]{1,0:T(8,128)(2,1)S(1)}, bf16[144,256]{1,0:T(8,128)(2,1)S(1)}, u32[]{:S(2)}, u32[]{:S(2)}) collective-permute-start(bf16[144,256]{1,0:T(8,128)(2,1)S(1)} %get-tuple-element.16), channel_id=1, source_target_pairs={{0,6},{1,7},{2,4},{3,5},{4,2},{5,3},{6,0},{7,1},{8,14},{9,15},{10,... | collective-permute-start | bytes 221192 | tf_op jit(solution)/shard_map/ppermute | solution.py:112
  22.1 0.7 %copy-start.3 = (f32[256]{0:T(256)S(1)}, f32[256]{0:T(256)}, u32[]{:S(2)}) copy-start(f32[256]{0:T(256)} %param.11) | copy-start | bytes 3076

commit v2 on v1

--- a/solution.py
+++ b/solution.py
@@ -10,7 +10,7 @@
 EXTRA = 16
 VMEM = pl.BlockSpec(memory_space=pltpu.VMEM)
 SMEM = pl.BlockSpec(memory_space=pltpu.SMEM)
-ANY = pl.BlockSpec(memory_space=pl.ANY)
+HBM = pl.BlockSpec(memory_space=pltpu.HBM)
 PARAMS = pltpu.CompilerParams(vmem_limit_bytes=32 * 1024 * 1024)
 
 
@@ -26,6 +26,14 @@
     return (index + count - step) % count
 
 
+def along_line(chip, step, chips):
+    odd = chip % 2
+    place = odd * (chips - 1) + (1 - 2 * odd) * (chip // 2)
+    place = (place + chips - step) % chips
+    back = place // ((chips + 1) // 2)
+    return back * (2 * (chips - 1 - place) + 1) + (1 - back) * 2 * place
+
+
 def split_rows(degree):
     high = degree.astype(jnp.bfloat16)
     low = (degree - high.astype(jnp.float32)).astype(jnp.bfloat16)
@@ -38,39 +46,77 @@
     return rows[:, :half] + rows[:, half:]
 
 
-def prepare_kernel(live, tiles, adjacency, degree):
+def group_order(chips):
+    chip, core = lax.axis_index("feat") // 2, lax.axis_index("feat") % 2
+    return [
+        along_line(chip, step, chips) * 2 + (core if mine else 1 - core)
+        for mine in range(2)
+        for step in range(chips)
+    ]
+
+
+def prepare_kernel(
+    live_in, src_in, tiles_in, feats_in, weight_in, bias_in,
+    adjacency, degree, chosen, feats, weight, bias,
+    live, src, tiles, tile_sems, sems,
+):
     groups, slots, tile, _ = tiles.shape
+    order = group_order(groups // 2)
+    small = [
+        pltpu.make_async_copy(live_in, live, sems.at[0]),
+        pltpu.make_async_copy(src_in, src, sems.at[1]),
+        pltpu.make_async_copy(feats_in, feats, sems.at[2]),
+        pltpu.make_async_copy(weight_in, weight, sems.at[3]),
+        pltpu.make_async_copy(bias_in, bias, sems.at[4]),
+    ]
+    large = [
+        pltpu.make_async_copy(tiles_in.at[group], tiles.at[place], tile_sems.at[place])
+        for place, group in enumerate(order)
+    ]
+    small[0].start()
+    small[1].start()
+    for copy in large:
+        copy.start()
+    for copy in small[2:]:
+        copy.start()
     ones = jnp.ones((EXTRA, slots * tile), jnp.bfloat16)
-    for group in range(groups):
-        count = live[group, 0]
+    small[0].wait()
+    small[1].wait()
+    for place, group in enumerate(order):
+        for slot in range(slots):
+            row = place * slots + slot
+            chosen[row : row + 1] = jnp.full((1, chosen.shape[1]), src[slot, group], jnp.int32)
+    for place, group in enumerate(order):
+        large[place].wait()
+        count = live[0, group]
         wide = []
         for slot in range(slots):
-            block = tiles[group, slot]
+            block = tiles[place, slot]
             wide.append(jnp.where(slot < count, block, jnp.zeros_like(block)))
         wide = jnp.concatenate(wide, axis=1)
-        adjacency[group] = wide
-        degree[group] = lax.dot_general(
+        adjacency[place] = wide
+        degree[place] = lax.dot_general(
             ones, wide, (((1,), (1,)), ((), ())), preferred_element_type=jnp.float32
         )
+    for copy in small[2:]:
+        copy.wait()
 
 
 def aggregate_kernel(nodes, chips, slots, mine, *refs):
-    src, adjacency, degree = refs[:3]
+    chosen, adjacency, degree = refs[:3]
     feats_in = refs[3 : 3 + nodes]
     out, rows = refs[3 + nodes :]
     node = lax.axis_index("node")
-    feat = lax.axis_index("feat")
-    chip = feat // 2
-    core = feat % 2 if mine else 1 - feat % 2
     tile = feats_in[0].shape[0]
     for step in range(nodes):
         rows[partner_back(node, step, nodes)] = feats_in[step][...]
     for step in range(chips):
-        group = partner(chip, step, chips) * 2 + core
-        right = jnp.concatenate([rows[src[group, slot]] for slot in range(slots)], axis=0)
-        product = jnp.dot(adjacency[group], right, preferred_element_type=jnp.float32)
+        place = mine * chips + step
+        picks = [chosen[place * slots + slot, 0] for slot in range(slots)]
+        right = jnp.concatenate([rows[pick] for pick in picks], axis=0)
+        product = jnp.dot(adjacency[place], right, preferred_element_type=jnp.float32)
         out[step, :tile] = product.astype(out.dtype)
-        out[step, tile:] = split_rows(degree[group]).astype(out.dtype)
+        out[step, tile:] = split_rows(degree[place]).astype(out.dtype)
 
 
 def merge_kernel(mine, theirs, own, *outs):
@@ -101,6 +147,7 @@
 def body(mesh, feats, tile_values, source_group, live_slots, proj_weight, proj_bias):
     nodes, chips = mesh.shape["node"], mesh.shape["feat"] // 2
     groups, slots = tile_values.shape[:2]
+    live_slots, source_group = live_slots.T, source_group.T
     tile, width = feats.shape
 
     def over_nodes(step):
@@ -108,36 +155,53 @@
         return lax.ppermute(feats, "node", pairs)
 
     def over_chips(array, step):
-        pairs = [(2 * z + c, 2 * partner(z, step, chips) + c) for z in range(chips) for c in range(2)]
+        pairs = [(2 * z + c, 2 * along_line(z, step, chips) + c) for z in range(chips) for c in range(2)]
         return lax.ppermute(array, "feat", pairs)
 
     def over_cores(array):
         return lax.ppermute(array, "feat", [(f, f ^ 1) for f in range(2 * chips)])
 
-    rows_in = [feats] + [over_nodes(step) for step in range(1, nodes)]
-    adjacency, degree = pl.pallas_call(
+    rows_in = [over_nodes(step) for step in range(1, nodes)]
+    adjacency, degree, chosen, own_feats, weight, bias = pl.pallas_call(
         prepare_kernel,
         out_shape=[
             jax.ShapeDtypeStruct((groups, tile, slots * tile), jnp.bfloat16),
             jax.ShapeDtypeStruct((groups, EXTRA, tile), jnp.float32),
+            jax.ShapeDtypeStruct((groups * slots, 128), jnp.int32),
+            jax.ShapeDtypeStruct(feats.shape, feats.dtype),
+            jax.ShapeDtypeStruct(proj_weight.shape, proj_weight.dtype),
+            jax.ShapeDtypeStruct((1, width), proj_bias.dtype),
         ],
-        in_specs=[SMEM, VMEM],
-        out_specs=[VMEM, VMEM],
+        in_specs=[HBM] * 6,
+        out_specs=[VMEM] * 6,
+        scratch_shapes=[
+            pltpu.SMEM(live_slots.shape, live_slots.dtype),
+            pltpu.SMEM(source_group.shape, source_group.dtype),
+            pltpu.VMEM(tile_values.shape, tile_values.dtype),
+            pltpu.SemaphoreType.DMA((groups,)),
+            pltpu.SemaphoreType.DMA((5,)),
+        ],
         compiler_params=PARAMS,
         cost_estimate=pl.CostEstimate(flops=1 << 27, bytes_accessed=1 << 22, transcendentals=0),
-    )(live_slots, tile_values)
+    )(
+        *(
+            pltpu.with_memory_space_constraint(array, pltpu.HBM)
+            for array in (live_slots, source_group, tile_values, feats, proj_weight, proj_bias.reshape(1, -1))
+        )
+    )
+    rows_in = [own_feats] + rows_in
 
     def aggregate(mine):
         dtype = jnp.float32 if mine else jnp.bfloat16
         return pl.pallas_call(
             functools.partial(aggregate_kernel, nodes, chips, slots, mine),
             out_shape=jax.ShapeDtypeStruct((chips, tile + EXTRA, width), dtype),
-            in_specs=[SMEM] + [VMEM] * (2 + nodes),
+            in_specs=[VMEM] * (3 + nodes),
             out_specs=VMEM,
             scratch_shapes=[pltpu.VMEM((nodes, tile, width), jnp.bfloat16)],
             compiler_params=PARAMS,
             cost_estimate=pl.CostEstimate(flops=1 << 27, bytes_accessed=1 << 22, transcendentals=0),
-        )(source_group, adjacency, degree, *rows_in)
+        )(chosen, adjacency, degree, *rows_in)
 
     theirs = over_cores(aggregate(False))
     own, *parts = pl.pallas_call(
@@ -155,7 +219,7 @@
         in_specs=[VMEM] * (chips + 3),
         out_specs=VMEM,
         compiler_params=PARAMS,
-    )(own, *parts, feats, proj_weight, proj_bias.reshape(1, -1))
+    )(own, *parts, own_feats, weight, bias)
 
 
 def solution(mesh):

time: 23.8 us -> 21.5 us (0.903)
  local copies, waits for them, and re-layouts: 2.66 us -> 0 us
  starting transfers between devices: 9.04 us -> 10.2 us
  waiting for transfers between devices: 8.04 us -> 6.91 us
  Pallas kernels: 3.82 us -> 4.19 us
    unnamed x12 -> x0, local copies, waits for them, and re-layouts: 2.66 us -> none
    ppermute x3, waiting for transfers between devices: 6.05 us -> 3.55 us  [over_chips(): return lax.ppermute(array, 'feat', pairs)]
    pallas_call x1, Pallas kernels: 1 us -> 2.54 us  [body(): pl.pallas_call(prepare_kernel, out_shape=[jax.ShapeDtypeStruct((groups, t...]
    ppermute x3, starting transfers between devices: 4.45 us -> 5.68 us  [over_chips(): return lax.ppermute(array, 'feat', pairs)]
    pallas_call x2, Pallas kernels: 1.88 us -> 0.7 us  [aggregate(): pl.pallas_call(functools.partial(aggregate_kernel, nodes, chips, slots, m...]
    ppermute x3, waiting for transfers between devices: 1.38 us -> 2.14 us  [over_nodes(): return lax.ppermute(feats, 'node', pairs)]
    ppermute x1, waiting for transfers between devices: 0.61 us -> 1.21 us  [over_cores(): return lax.ppermute(array, 'feat', [(f, f ^ 1) for f in range(2 * chips)])]
  transfers between devices with their start and end apart: 7 -> 7, of which waited for: 4 -> 5; matrix products, arithmetic and copies ran while one was open for 4% -> 0% of each run, Pallas kernels for 8% -> 14%
where the time goes in v2:
time: 21.5 us; the launch traced here: 21.4 us
  starting transfers between devices  10.2 us (47%)
  waiting for transfers between devices  6.91 us (32%)
  Pallas kernels  4.19 us (19%)
    ppermute x3, starting transfers between devices, over_chips(): return lax.ppermute(array, 'feat', pairs)  5.68 us
    ppermute x3, starting transfers between devices, over_nodes(): return lax.ppermute(feats, 'node', pairs)  4.46 us
    ppermute x3, waiting for transfers between devices, over_chips(): return lax.ppermute(array, 'feat', pairs)  3.55 us
    pallas_call x1, Pallas kernels, body(): pl.pallas_call(prepare_kernel, out_shape=[jax.ShapeDtypeStruct((groups, t...  2.54 us
    ppermute x3, waiting for transfers between devices, over_nodes(): return lax.ppermute(feats, 'node', pairs)  2.14 us
    ppermute x1, waiting for transfers between devices, over_cores(): return lax.ppermute(array, 'feat', [(f, f ^ 1) for f in range(2 * chips)])  1.21 us
    pallas_call x1, Pallas kernels, body(): pl.pallas_call(update_kernel, out_shape=jax.ShapeDtypeStruct((tile, width...  0.87 us
    pallas_call x2, Pallas kernels, aggregate(): pl.pallas_call(functools.partial(aggregate_kernel, nodes, chips, slots, m...  0.7 us
  transfers between devices with their start and end apart: 7, of which 5 were waited for; matrix products, arithmetic and copies ran while one was open for 0% of the time, Pallas kernels for 14%

profile of v2, /device:TPU:0, one launch (start us, length us, event | category | flops | bytes accessed | tf_op | source)
XLA Modules:
  0.0 21.4 jit_solution(9003478826213010396)
XLA Ops:
  0.0 2.9 %collective-permute-start = (bf16[128,256]{1,0:T(8,128)(2,1)}, bf16[128,256]{1,0:T(8,128)(2,1)S(1)}, u32[]{:S(2)}, u32[]{:S(2)}) collective-permute-start(bf16[128,256]{1,0:T(8,128)(2,1)} %feats_in.1), channel_id=1, source_target_pairs={{0,8},{8,0},{16,24},{24,16},{1,9},{9,1},{17,25},{25,17},{2,10},{10... | collective-permute-start | bytes 196616 | tf_op jit(solution)/shard_map/ppermute | solution.py:155
  2.9 1.5 %collective-permute-start.2 = (bf16[128,256]{1,0:T(8,128)(2,1)}, bf16[128,256]{1,0:T(8,128)(2,1)S(1)}, u32[]{:S(2)}, u32[]{:S(2)}) collective-permute-start(bf16[128,256]{1,0:T(8,128)(2,1)} %feats_in.1), channel_id=1, source_target_pairs={{0,24},{8,16},{16,8},{24,0},{1,25},{9,17},{17,9},{25,1},{2,26},{10... | collective-permute-start | bytes 196616 | tf_op jit(solution)/shard_map/ppermute | solution.py:155
  4.4 0.0 collective-permute-start.1
  4.5 2.5 %shard_map.64 = (bf16[8,128,384]{2,1,0:T(8,128)(2,1)S(1)}, f32[8,16,128]{2,1,0:T(8,128)S(1)}, s32[24,128]{1,0:T(8,128)S(1)}, bf16[128,256]{1,0:T(8,128)(2,1)S(1)...) custom-call(s32[1,8]{1,0:T(1,128)} %bitcast.5, s32[3,8]{1,0:T(4,128)} %bitcast.3, ...), custom_call_target="tpu_custom_call" | custom-call | flops 134217728 | bytes 4194304 | tf_op jit(solution)/shard_map/pallas_call | solution.py:165
  7.0 0.0 collective-permute-done.refs_4_
  7.0 1.4 %collective-permute-done.2.refs_6_ = bf16[128,256]{1,0:T(8,128)(2,1)S(1)} collective-permute-done((bf16[128,256]{1,0:T(8,128)(2,1)}, bf16[128,256]{1,0:T(8,128)(2,1)S(1)}, u32[]{:S(2)}, u32[]{:S(2)}) %collective-permute-start.2) | collective-permute-done | bytes 65568 | tf_op jit(solution)/shard_map/ppermute | solution.py:155
  8.4 0.8 %collective-permute-done.1.refs_5_ = bf16[128,256]{1,0:T(8,128)(2,1)S(1)} collective-permute-done((bf16[128,256]{1,0:T(8,128)(2,1)}, bf16[128,256]{1,0:T(8,128)(2,1)S(1)}, u32[]{:S(2)}, u32[]{:S(2)}) %collective-permute-start.1) | collective-permute-done | bytes 65568 | tf_op jit(solution)/shard_map/ppermute | solution.py:155
  9.2 0.3 %shard_map.66 = bf16[4,144,256]{2,1,0:T(8,128)(2,1)S(1)} custom-call(s32[24,128]{1,0:T(8,128)S(1)} %get-tuple-element.15.refs_0_, bf16[8,128,384]{2,1,0:T(8,128)(2,1)S(1)} %get-tuple-element.16.refs_1_, f32[8,16,128]{2,1,0:T(8,128)S(1)} %get-tuple-element.17.refs_2_, bf16[128,256]{1,0:T(8,128)(2,1)S(1)} %get-tuple-element.18.refs_3_.refs_4_, ...), custom_call_target="tpu_custom_call" | custom-call | flops 134217728 | bytes 4194304 | tf_op jit(solution)/shard_map/pallas_call | solution.py:196
  9.5 0.1 collective-permute-start.3
  9.6 0.3 %shard_map.65.mine = f32[4,144,256]{2,1,0:T(8,128)S(1)} custom-call(s32[24,128]{1,0:T(8,128)S(1)} %get-tuple-element.15.refs_0_, bf16[8,128,384]{2,1,0:T(8,128)(2,1)S(1)} %get-tuple-element.16.refs_1_, f32[8,16,128]{2,1,0:T(8,128)S(1)} %get-tuple-element.17.refs_2_, bf16[128,256]{1,0:T(8,128)(2,1)S(1)} %get-tuple-element.18.refs_3_.refs_4_, ...), custom_call_target="tpu_custom_call" | custom-call | flops 134217728 | bytes 4194304 | tf_op jit(solution)/shard_map/pallas_call | solution.py:196
  10.0 1.2 %collective-permute-done.3.theirs = bf16[4,144,256]{2,1,0:T(8,128)(2,1)S(1)} collective-permute-done((bf16[4,144,256]{2,1,0:T(8,128)(2,1)S(1)}, bf16[4,144,256]{2,1,0:T(8,128)(2,1)S(1)}, u32[]{:S(2)}, u32[]{:S(2)}) %collective-permute-start.3) | collective-permute-done | bytes 294944 | tf_op jit(solution)/shard_map/ppermute | solution.py:162
  11.2 0.1 shard_map.67
  11.2 1.6 %collective-permute-start.4 = (bf16[144,256]{1,0:T(8,128)(2,1)S(1)}, bf16[144,256]{1,0:T(8,128)(2,1)S(1)}, u32[]{:S(2)}, u32[]{:S(2)}) collective-permute-start(bf16[144,256]{1,0:T(8,128)(2,1)S(1)} %get-tuple-element.20), channel_id=1, source_target_pairs={{0,2},{1,3},{2,6},{3,7},{4,0},{5,1},{6,4},{7,5},{8,10},{9,11},{10,... | collective-permute-start | bytes 221192 | tf_op jit(solution)/shard_map/ppermute | solution.py:159
  12.9 2.5 %collective-permute-start.5 = (bf16[144,256]{1,0:T(8,128)(2,1)S(1)}, bf16[144,256]{1,0:T(8,128)(2,1)S(1)}, u32[]{:S(2)}, u32[]{:S(2)}) collective-permute-start(bf16[144,256]{1,0:T(8,128)(2,1)S(1)} %get-tuple-element.21), channel_id=1, source_target_pairs={{0,6},{1,7},{2,4},{3,5},{4,2},{5,3},{6,0},{7,1},{8,14},{9,15},{10,... | collective-permute-start | bytes 221192 | tf_op jit(solution)/shard_map/ppermute | solution.py:159
  15.3 1.6 %collective-permute-start.6 = (bf16[144,256]{1,0:T(8,128)(2,1)S(1)}, bf16[144,256]{1,0:T(8,128)(2,1)S(1)}, u32[]{:S(2)}, u32[]{:S(2)}) collective-permute-start(bf16[144,256]{1,0:T(8,128)(2,1)S(1)} %get-tuple-element.22), channel_id=1, source_target_pairs={{0,4},{1,5},{2,0},{3,1},{4,6},{5,7},{6,2},{7,3},{8,12},{9,13},{10,... | collective-permute-start | bytes 221192 | tf_op jit(solution)/shard_map/ppermute | solution.py:159
  16.9 0.0 collective-permute-done.4.refs_1_
  16.9 3.0 %collective-permute-done.5.refs_2_ = bf16[144,256]{1,0:T(8,128)(2,1)S(1)} collective-permute-done((bf16[144,256]{1,0:T(8,128)(2,1)S(1)}, bf16[144,256]{1,0:T(8,128)(2,1)S(1)}, u32[]{:S(2)}, u32[]{:S(2)}) %collective-permute-start.5) | collective-permute-done | bytes 73760 | tf_op jit(solution)/shard_map/ppermute | solution.py:159
  19.9 0.6 %collective-permute-done.6.refs_3_ = bf16[144,256]{1,0:T(8,128)(2,1)S(1)} collective-permute-done((bf16[144,256]{1,0:T(8,128)(2,1)S(1)}, bf16[144,256]{1,0:T(8,128)(2,1)S(1)}, u32[]{:S(2)}, u32[]{:S(2)}) %collective-permute-start.6) | collective-permute-done | bytes 73760 | tf_op jit(solution)/shard_map/ppermute | solution.py:159
  20.5 0.9 %shard_map.68 = bf16[128,256]{1,0:T(8,128)(2,1)} custom-call(f32[144,256]{1,0:T(8,128)S(1)} %get-tuple-element.19.refs_0_, bf16[144,256]{1,0:T(8,128)(2,1)S(1)} %collective-permute-done.4.refs_1_, bf16[144,256]{1,0:T(8,128)(2,1)S(1)} %collective-permute-done.5.refs_2_, bf16[144,256]{1,0:T(8,128)(2,1)S(1)} %collective-permute-done.6.refs_3_, ...), custom_call_target="tpu_custom_call" | custom-call | tf_op jit(solution)/shard_map/pallas_call | solution.py:216
Async XLA Ops:
  0.0 7.0 %collective-permute-start = (bf16[128,256]{1,0:T(8,128)(2,1)}, bf16[128,256]{1,0:T(8,128)(2,1)S(1)}, u32[]{:S(2)}, u32[]{:S(2)}) collective-permute-start(bf16[128,256]{1,0:T(8,128)(2,1)} %feats_in.1), channel_id=1, source_target_pairs={{0,8},{8,0},{16,24},{24,16},{1,9},{9,1},{17,25},{25,17},{2,10},{10... | collective-permute-start | bytes 196616 | tf_op jit(solution)/shard_map/ppermute | solution.py:155
  2.9 5.4 %collective-permute-start.2 = (bf16[128,256]{1,0:T(8,128)(2,1)}, bf16[128,256]{1,0:T(8,128)(2,1)S(1)}, u32[]{:S(2)}, u32[]{:S(2)}) collective-permute-start(bf16[128,256]{1,0:T(8,128)(2,1)} %feats_in.1), channel_id=1, source_target_pairs={{0,24},{8,16},{16,8},{24,0},{1,25},{9,17},{17,9},{25,1},{2,26},{10... | collective-permute-start | bytes 196616 | tf_op jit(solution)/shard_map/ppermute | solution.py:155
  4.4 4.7 %collective-permute-start.1 = (bf16[128,256]{1,0:T(8,128)(2,1)}, bf16[128,256]{1,0:T(8,128)(2,1)S(1)}, u32[]{:S(2)}, u32[]{:S(2)}) collective-permute-start(bf16[128,256]{1,0:T(8,128)(2,1)} %feats_in.1), channel_id=1, source_target_pairs={{0,16},{8,24},{16,0},{24,8},{1,17},{9,25},{17,1},{25,9},{2,18},{10... | collective-permute-start | bytes 196616 | tf_op jit(solution)/shard_map/ppermute | solution.py:155
  9.5 1.6 %collective-permute-start.3 = (bf16[4,144,256]{2,1,0:T(8,128)(2,1)S(1)}, bf16[4,144,256]{2,1,0:T(8,128)(2,1)S(1)}, u32[]{:S(2)}, u32[]{:S(2)}) collective-permute-start(bf16[4,144,256]{2,1,0:T(8,128)(2,1)S(1)} %shard_map.66), channel_id=1, source_target_pairs={{0,1},{1,0},{2,3},{3,2},{4,5},{5,4},{6,7},{7,6},{8,9},{9,8},{10,11... | collective-permute-start | bytes 884744 | tf_op jit(solution)/shard_map/ppermute | solution.py:162
  11.2 5.7 %collective-permute-start.4 = (bf16[144,256]{1,0:T(8,128)(2,1)S(1)}, bf16[144,256]{1,0:T(8,128)(2,1)S(1)}, u32[]{:S(2)}, u32[]{:S(2)}) collective-permute-start(bf16[144,256]{1,0:T(8,128)(2,1)S(1)} %get-tuple-element.20), channel_id=1, source_target_pairs={{0,2},{1,3},{2,6},{3,7},{4,0},{5,1},{6,4},{7,5},{8,10},{9,11},{10,... | collective-permute-start | bytes 221192 | tf_op jit(solution)/shard_map/ppermute | solution.py:159
  12.9 7.1 %collective-permute-start.5 = (bf16[144,256]{1,0:T(8,128)(2,1)S(1)}, bf16[144,256]{1,0:T(8,128)(2,1)S(1)}, u32[]{:S(2)}, u32[]{:S(2)}) collective-permute-start(bf16[144,256]{1,0:T(8,128)(2,1)S(1)} %get-tuple-element.21), channel_id=1, source_target_pairs={{0,6},{1,7},{2,4},{3,5},{4,2},{5,3},{6,0},{7,1},{8,14},{9,15},{10,... | collective-permute-start | bytes 221192 | tf_op jit(solution)/shard_map/ppermute | solution.py:159
  15.3 5.1 %collective-permute-start.6 = (bf16[144,256]{1,0:T(8,128)(2,1)S(1)}, bf16[144,256]{1,0:T(8,128)(2,1)S(1)}, u32[]{:S(2)}, u32[]{:S(2)}) collective-permute-start(bf16[144,256]{1,0:T(8,128)(2,1)S(1)} %get-tuple-element.22), channel_id=1, source_target_pairs={{0,4},{1,5},{2,0},{3,1},{4,6},{5,7},{6,2},{7,3},{8,12},{9,13},{10,... | collective-permute-start | bytes 221192 | tf_op jit(solution)/shard_map/ppermute | solution.py:159

commit v3 on v2

--- a/solution.py
+++ b/solution.py
@@ -7,31 +7,20 @@
 from jax.experimental.pallas import tpu as pltpu
 from jax.sharding import PartitionSpec as P
 
-EXTRA = 16
+EXTRA = 8
+FIRST = 2
 VMEM = pl.BlockSpec(memory_space=pltpu.VMEM)
 SMEM = pl.BlockSpec(memory_space=pltpu.SMEM)
 HBM = pl.BlockSpec(memory_space=pltpu.HBM)
 PARAMS = pltpu.CompilerParams(vmem_limit_bytes=32 * 1024 * 1024)
 
 
-def partner(index, step, count):
-    if count & (count - 1) == 0:
-        return index ^ step
-    return (index + step) % count
-
-
-def partner_back(index, step, count):
-    if count & (count - 1) == 0:
-        return index ^ step
-    return (index + count - step) % count
-
-
-def along_line(chip, step, chips):
-    odd = chip % 2
-    place = odd * (chips - 1) + (1 - 2 * odd) * (chip // 2)
-    place = (place + chips - step) % chips
-    back = place // ((chips + 1) // 2)
-    return back * (2 * (chips - 1 - place) + 1) + (1 - back) * 2 * place
+def along_ring(index, step, count):
+    odd = index % 2
+    place = odd * (count - 1) + (1 - 2 * odd) * (index // 2)
+    place = (place + count - step) % count
+    back = place // ((count + 1) // 2)
+    return back * (2 * (count - 1 - place) + 1) + (1 - back) * 2 * place
 
 
 def split_rows(degree):
@@ -49,7 +38,7 @@
 def group_order(chips):
     chip, core = lax.axis_index("feat") // 2, lax.axis_index("feat") % 2
     return [
-        along_line(chip, step, chips) * 2 + (core if mine else 1 - core)
+        along_ring(chip, step, chips) * 2 + (core if mine else 1 - core)
         for mine in range(2)
         for step in range(chips)
     ]
@@ -102,29 +91,28 @@
         copy.wait()
 
 
-def aggregate_kernel(nodes, chips, slots, mine, *refs):
+def aggregate_kernel(nodes, chips, slots, mine, steps, *refs):
     chosen, adjacency, degree = refs[:3]
     feats_in = refs[3 : 3 + nodes]
     out, rows = refs[3 + nodes :]
     node = lax.axis_index("node")
     tile = feats_in[0].shape[0]
     for step in range(nodes):
-        rows[partner_back(node, step, nodes)] = feats_in[step][...]
-    for step in range(chips):
+        rows[along_ring(node, (nodes - step) % nodes, nodes)] = feats_in[step][...]
+    for index, step in enumerate(steps):
         place = mine * chips + step
         picks = [chosen[place * slots + slot, 0] for slot in range(slots)]
         right = jnp.concatenate([rows[pick] for pick in picks], axis=0)
         product = jnp.dot(adjacency[place], right, preferred_element_type=jnp.float32)
-        out[step, :tile] = product.astype(out.dtype)
-        out[step, tile:] = split_rows(degree[place]).astype(out.dtype)
-
-
-def merge_kernel(mine, theirs, own, *outs):
+        out[index, :tile] = product.astype(out.dtype)
+        out[index, tile:] = split_rows(degree[place]).astype(out.dtype)
+
+
+def merge_kernel(mine, theirs, *outs):
     tile = mine.shape[1] - EXTRA
-    for step in range(mine.shape[0]):
-        total = mine[step, :tile] + theirs[step, :tile].astype(jnp.float32)
-        degree = split_rows(join_rows(mine[step, tile:]) + join_rows(theirs[step, tile:]))
-        out = outs[step - 1] if step else own
+    for index, out in enumerate(outs):
+        total = mine[index, :tile] + theirs[index, :tile].astype(jnp.float32)
+        degree = split_rows(join_rows(mine[index, tile:]) + join_rows(theirs[index, tile:]))
         out[:tile] = total.astype(out.dtype)
         out[tile:] = degree.astype(out.dtype)
 
@@ -151,11 +139,11 @@
     tile, width = feats.shape
 
     def over_nodes(step):
-        pairs = [(n, partner(n, step, nodes)) for n in range(nodes)]
+        pairs = [(n, along_ring(n, step, nodes)) for n in range(nodes)]
         return lax.ppermute(feats, "node", pairs)
 
     def over_chips(array, step):
-        pairs = [(2 * z + c, 2 * along_line(z, step, chips) + c) for z in range(chips) for c in range(2)]
+        pairs = [(2 * z + c, 2 * along_ring(z, step, chips) + c) for z in range(chips) for c in range(2)]
         return lax.ppermute(array, "feat", pairs)
 
     def over_cores(array):
@@ -191,11 +179,11 @@
     )
     rows_in = [own_feats] + rows_in
 
-    def aggregate(mine):
+    def aggregate(mine, steps):
         dtype = jnp.float32 if mine else jnp.bfloat16
         return pl.pallas_call(
-            functools.partial(aggregate_kernel, nodes, chips, slots, mine),
-            out_shape=jax.ShapeDtypeStruct((chips, tile + EXTRA, width), dtype),
+            functools.partial(aggregate_kernel, nodes, chips, slots, mine, steps),
+            out_shape=jax.ShapeDtypeStruct((len(steps), tile + EXTRA, width), dtype),
             in_specs=[VMEM] * (3 + nodes),
             out_specs=VMEM,
             scratch_shapes=[pltpu.VMEM((nodes, tile, width), jnp.bfloat16)],
@@ -203,16 +191,22 @@
             cost_estimate=pl.CostEstimate(flops=1 << 27, bytes_accessed=1 << 22, transcendentals=0),
         )(chosen, adjacency, degree, *rows_in)
 
-    theirs = over_cores(aggregate(False))
-    own, *parts = pl.pallas_call(
-        merge_kernel,
-        out_shape=[jax.ShapeDtypeStruct((tile + EXTRA, width), jnp.float32)]
-        + [jax.ShapeDtypeStruct((tile + EXTRA, width), jnp.bfloat16)] * (chips - 1),
-        in_specs=[VMEM] * 2,
-        out_specs=[VMEM] * chips,
-        compiler_params=PARAMS,
-    )(aggregate(True), theirs)
-    parts = [over_chips(part, step) for step, part in enumerate(parts, 1)]
+    def merge(mine, theirs, dtypes):
+        return pl.pallas_call(
+            merge_kernel,
+            out_shape=[jax.ShapeDtypeStruct((tile + EXTRA, width), dtype) for dtype in dtypes],
+            in_specs=[VMEM] * 2,
+            out_specs=[VMEM] * len(dtypes),
+            compiler_params=PARAMS,
+        )(mine, theirs)
+
+    cut = min(chips, FIRST + 1)
+    far, near = list(range(1, cut)), list(range(cut, chips)) + [0]
+    theirs_far = over_cores(aggregate(0, far))
+    theirs_near = over_cores(aggregate(0, near))
+    parts = merge(aggregate(1, far), theirs_far, [jnp.bfloat16] * len(far))
+    *rest, own = merge(aggregate(1, near), theirs_near, [jnp.bfloat16] * (len(near) - 1) + [jnp.float32])
+    parts = [over_chips(part, step) for step, part in enumerate([*parts, *rest], 1)]
     return pl.pallas_call(
         update_kernel,
         out_shape=jax.ShapeDtypeStruct((tile, width), jnp.bfloat16),

time: 21.5 us -> 20.8 us (0.967)
  waiting for transfers between devices: 6.91 us -> 3.64 us
  starting transfers between devices: 10.2 us -> 12.3 us
  Pallas kernels: 4.19 us -> 4.67 us
    ppermute x3, waiting for transfers between devices: 2.14 us -> 0.42 us  [over_nodes(): return lax.ppermute(feats, 'node', pairs)]
    ppermute x3, starting transfers between devices: 4.46 us -> 5.92 us  [over_nodes(): return lax.ppermute(feats, 'node', pairs)]
    ppermute x1 -> x2, waiting for transfers between devices: 1.21 us -> 0.01 us  [over_cores(): return lax.ppermute(array, 'feat', [(f, f ^ 1) for f in range(2 * chips)])]
    ppermute x1 -> x2, starting transfers between devices: 0.07 us -> 0.63 us  [over_cores(): return lax.ppermute(array, 'feat', [(f, f ^ 1) for f in range(2 * chips)])]
    pallas_call x2 -> x4, Pallas kernels: 0.7 us -> 1.17 us  [aggregate(): pl.pallas_call(functools.partial(aggregate_kernel, nodes, chips, slots, m...]
    ppermute x3, waiting for transfers between devices: 3.55 us -> 3.22 us  [over_chips(): return lax.ppermute(array, 'feat', pairs)]
  transfers between devices with their start and end apart: 7 -> 8, of which waited for: 5 -> 3; matrix products, arithmetic and copies ran while one was open for 0% -> 0% of each run, Pallas kernels for 14% -> 17%
where the time goes in v3:
time: 20.8 us; the launch traced here: 20.7 us
  starting transfers between devices  12.3 us (59%)
  Pallas kernels  4.67 us (22%)
  waiting for transfers between devices  3.64 us (18%)
    ppermute x3, starting transfers between devices, over_nodes(): return lax.ppermute(feats, 'node', pairs)  5.92 us
    ppermute x3, starting transfers between devices, over_chips(): return lax.ppermute(array, 'feat', pairs)  5.73 us
    ppermute x3, waiting for transfers between devices, over_chips(): return lax.ppermute(array, 'feat', pairs)  3.22 us
    pallas_call x1, Pallas kernels, body(): pl.pallas_call(prepare_kernel, out_shape=[jax.ShapeDtypeStruct((groups, t...  2.54 us
    pallas_call x4, Pallas kernels, aggregate(): pl.pallas_call(functools.partial(aggregate_kernel, nodes, chips, slots, m...  1.17 us
    pallas_call x1, Pallas kernels, body(): pl.pallas_call(update_kernel, out_shape=jax.ShapeDtypeStruct((tile, width...  0.87 us
    ppermute x2, starting transfers between devices, over_cores(): return lax.ppermute(array, 'feat', [(f, f ^ 1) for f in range(2 * chips)])  0.63 us
    ppermute x3, waiting for transfers between devices, over_nodes(): return lax.ppermute(feats, 'node', pairs)  0.42 us
  transfers between devices with their start and end apart: 8, of which 3 were waited for; matrix products, arithmetic and copies ran while one was open for 0% of the time, Pallas kernels for 17%

profile of v3, /device:TPU:0, one launch (start us, length us, event | category | flops | bytes accessed | tf_op | source)
XLA Modules:
  0.0 20.7 jit_solution(2653374557939808349)
XLA Ops:
  0.0 2.9 %collective-permute-start = (bf16[128,256]{1,0:T(8,128)(2,1)}, bf16[128,256]{1,0:T(8,128)(2,1)S(1)}, u32[]{:S(2)}, u32[]{:S(2)}) collective-permute-start(bf16[128,256]{1,0:T(8,128)(2,1)} %feats_in.1), channel_id=1, source_target_pairs={{0,8},{8,24},{16,0},{24,16},{1,9},{9,25},{17,1},{25,17},{2,10},{10... | collective-permute-start | bytes 196616 | tf_op jit(solution)/shard_map/ppermute | solution.py:143
  2.9 1.5 %collective-permute-start.1 = (bf16[128,256]{1,0:T(8,128)(2,1)}, bf16[128,256]{1,0:T(8,128)(2,1)S(1)}, u32[]{:S(2)}, u32[]{:S(2)}) collective-permute-start(bf16[128,256]{1,0:T(8,128)(2,1)} %feats_in.1), channel_id=1, source_target_pairs={{0,24},{8,16},{16,8},{24,0},{1,25},{9,17},{17,9},{25,1},{2,26},{10... | collective-permute-start | bytes 196616 | tf_op jit(solution)/shard_map/ppermute | solution.py:143
  4.4 1.5 %collective-permute-start.2 = (bf16[128,256]{1,0:T(8,128)(2,1)}, bf16[128,256]{1,0:T(8,128)(2,1)S(1)}, u32[]{:S(2)}, u32[]{:S(2)}) collective-permute-start(bf16[128,256]{1,0:T(8,128)(2,1)} %feats_in.1), channel_id=1, source_target_pairs={{0,16},{8,0},{16,24},{24,8},{1,17},{9,1},{17,25},{25,9},{2,18},{10... | collective-permute-start | bytes 196616 | tf_op jit(solution)/shard_map/ppermute | solution.py:143
  5.9 2.5 %shard_map.64 = (bf16[8,128,384]{2,1,0:T(8,128)(2,1)S(1)}, f32[8,8,128]{2,1,0:T(8,128)S(1)}, s32[24,128]{1,0:T(8,128)S(1)}, bf16[128,256]{1,0:T(8,128)(2,1)S(1)}...) custom-call(s32[1,8]{1,0:T(1,128)} %bitcast.5, s32[3,8]{1,0:T(4,128)} %bitcast.3, bf16[8,3,128,128]{3,2,1,0:T(8,128)(2,1)} %tiles_in.1, ...), custom_call_target="tpu_custom_call" | custom-call | flops 134217728 | bytes 4194304 | tf_op jit(solution)/shard_map/pallas_call | solution.py:153
  8.5 0.0 collective-permute-done.refs_4_
  8.5 0.0 collective-permute-done.1.refs_5_
  8.5 0.4 %collective-permute-done.2.refs_6_ = bf16[128,256]{1,0:T(8,128)(2,1)S(1)} collective-permute-done((bf16[128,256]{1,0:T(8,128)(2,1)}, bf16[128,256]{1,0:T(8,128)(2,1)S(1)}, u32[]{:S(2)}, u32[]{:S(2)}) %collective-permute-start.2) | collective-permute-done | bytes 65568 | tf_op jit(solution)/shard_map/ppermute | solution.py:143
  8.9 0.3 %shard_map.69 = bf16[2,136,256]{2,1,0:T(8,128)(2,1)S(1)} custom-call(s32[24,128]{1,0:T(8,128)S(1)} %get-tuple-element.15.refs_0_, bf16[8,128,384]{2,1,0:T(8,128)(2,1)S(1)} %get-tuple-element.16.refs_1_, f32[8,8,128]{2,1,0:T(8,128)S(1)} %get-tuple-element.17.refs_2_, bf16[128,256]{1,0:T(8,128)(2,1)S(1)} %get-tuple-element.18.refs_3_.refs_4_, ...), custom_call_target="tpu_custom_call" | custom-call | flops 134217728 | bytes 4194304 | tf_op jit(solution)/shard_map/pallas_call | solution.py:184
  9.2 0.1 collective-permute-start.4
  9.3 0.3 %shard_map.66 = bf16[2,136,256]{2,1,0:T(8,128)(2,1)S(1)} custom-call(s32[24,128]{1,0:T(8,128)S(1)} %get-tuple-element.15.refs_0_, bf16[8,128,384]{2,1,0:T(8,128)(2,1)S(1)} %get-tuple-element.16.refs_1_, f32[8,8,128]{2,1,0:T(8,128)S(1)} %get-tuple-element.17.refs_2_, bf16[128,256]{1,0:T(8,128)(2,1)S(1)} %get-tuple-element.18.refs_3_.refs_4_, ...), custom_call_target="tpu_custom_call" | custom-call | flops 134217728 | bytes 4194304 | tf_op jit(solution)/shard_map/pallas_call | solution.py:184
  9.6 0.6 %collective-permute-start.3 = (bf16[2,136,256]{2,1,0:T(8,128)(2,1)S(1)}, bf16[2,136,256]{2,1,0:T(8,128)(2,1)S(1)}, u32[]{:S(2)}, u32[]{:S(2)}) collective-permute-start(bf16[2,136,256]{2,1,0:T(8,128)(2,1)S(1)} %shard_map.66), channel_id=1, source_target_pairs={{0,1},{1,0},{2,3},{3,2},{4,5},{5,4},{6,7},{7,6},{8,9},{9,8},{10,11... | collective-permute-start | bytes 417800 | tf_op jit(solution)/shard_map/ppermute | solution.py:150
  10.1 0.3 %shard_map.68.mine = f32[2,136,256]{2,1,0:T(8,128)S(1)} custom-call(s32[24,128]{1,0:T(8,128)S(1)} %get-tuple-element.15.refs_0_, bf16[8,128,384]{2,1,0:T(8,128)(2,1)S(1)} %get-tuple-element.16.refs_1_, f32[8,8,128]{2,1,0:T(8,128)S(1)} %get-tuple-element.17.refs_2_, bf16[128,256]{1,0:T(8,128)(2,1)S(1)} %get-tuple-element.18.refs_3_.refs_4_, ...), custom_call_target="tpu_custom_call" | custom-call | flops 134217728 | bytes 4194304 | tf_op jit(solution)/shard_map/pallas_call | solution.py:184
  10.4 0.3 %shard_map.65.mine = f32[2,136,256]{2,1,0:T(8,128)S(1)} custom-call(s32[24,128]{1,0:T(8,128)S(1)} %get-tuple-element.15.refs_0_, bf16[8,128,384]{2,1,0:T(8,128)(2,1)S(1)} %get-tuple-element.16.refs_1_, f32[8,8,128]{2,1,0:T(8,128)S(1)} %get-tuple-element.17.refs_2_, bf16[128,256]{1,0:T(8,128)(2,1)S(1)} %get-tuple-element.18.refs_3_.refs_4_, ...), custom_call_target="tpu_custom_call" | custom-call | flops 134217728 | bytes 4194304 | tf_op jit(solution)/shard_map/pallas_call | solution.py:184
  10.7 0.0 collective-permute-done.4.theirs
  10.8 1.6 %collective-permute-start.5 = (bf16[136,256]{1,0:T(8,128)(2,1)S(1)}, bf16[136,256]{1,0:T(8,128)(2,1)S(1)}, u32[]{:S(2)}, u32[]{:S(2)}) collective-permute-start(bf16[136,256]{1,0:T(8,128)(2,1)S(1)} %get-tuple-element.20), channel_id=1, source_target_pairs={{0,2},{1,3},{2,6},{3,7},{4,0},{5,1},{6,4},{7,5},{8,10},{9,11},{10,... | collective-permute-start | bytes 208904 | tf_op jit(solution)/shard_map/ppermute | solution.py:147
  12.4 2.5 %collective-permute-start.6 = (bf16[136,256]{1,0:T(8,128)(2,1)S(1)}, bf16[136,256]{1,0:T(8,128)(2,1)S(1)}, u32[]{:S(2)}, u32[]{:S(2)}) collective-permute-start(bf16[136,256]{1,0:T(8,128)(2,1)S(1)} %get-tuple-element.21), channel_id=1, source_target_pairs={{0,6},{1,7},{2,4},{3,5},{4,2},{5,3},{6,0},{7,1},{8,14},{9,15},{10,... | collective-permute-start | bytes 208904 | tf_op jit(solution)/shard_map/ppermute | solution.py:147
  14.9 0.0 collective-permute-done.3.theirs
  14.9 1.6 %collective-permute-start.7 = (bf16[136,256]{1,0:T(8,128)(2,1)S(1)}, bf16[136,256]{1,0:T(8,128)(2,1)S(1)}, u32[]{:S(2)}, u32[]{:S(2)}) collective-permute-start(bf16[136,256]{1,0:T(8,128)(2,1)S(1)} %get-tuple-element.22), channel_id=1, source_target_pairs={{0,4},{1,5},{2,0},{3,1},{4,6},{5,7},{6,2},{7,3},{8,12},{9,13},{10,... | collective-permute-start | bytes 208904 | tf_op jit(solution)/shard_map/ppermute | solution.py:147
  16.6 0.0 collective-permute-done.5.refs_1_
  16.6 2.8 %collective-permute-done.6.refs_2_ = bf16[136,256]{1,0:T(8,128)(2,1)S(1)} collective-permute-done((bf16[136,256]{1,0:T(8,128)(2,1)S(1)}, bf16[136,256]{1,0:T(8,128)(2,1)S(1)}, u32[]{:S(2)}, u32[]{:S(2)}) %collective-permute-start.6) | collective-permute-done | bytes 69664 | tf_op jit(solution)/shard_map/ppermute | solution.py:147
  19.4 0.4 %collective-permute-done.7.refs_3_ = bf16[136,256]{1,0:T(8,128)(2,1)S(1)} collective-permute-done((bf16[136,256]{1,0:T(8,128)(2,1)S(1)}, bf16[136,256]{1,0:T(8,128)(2,1)S(1)}, u32[]{:S(2)}, u32[]{:S(2)}) %collective-permute-start.7) | collective-permute-done | bytes 69664 | tf_op jit(solution)/shard_map/ppermute | solution.py:147
  19.8 0.9 %shard_map.71 = bf16[128,256]{1,0:T(8,128)(2,1)} custom-call(f32[136,256]{1,0:T(8,128)S(1)} %get-tuple-element.19.refs_0_, bf16[136,256]{1,0:T(8,128)(2,1)S(1)} %collective-permute-done.5.refs_1_, bf16[136,256]{1,0:T(8,128)(2,1)S(1)} %collective-permute-done.6.refs_2_, bf16[136,256]{1,0:T(8,128)(2,1)S(1)} %collective-permute-done.7.refs_3_, ...), custom_call_target="tpu_custom_call" | custom-call | tf_op jit(solution)/shard_map/pallas_call | solution.py:210
  (2 shorter events, 0.1 us)
Async XLA Ops:
  0.0 8.5 %collective-permute-start = (bf16[128,256]{1,0:T(8,128)(2,1)}, bf16[128,256]{1,0:T(8,128)(2,1)S(1)}, u32[]{:S(2)}, u32[]{:S(2)}) collective-permute-start(bf16[128,256]{1,0:T(8,128)(2,1)} %feats_in.1), channel_id=1, source_target_pairs={{0,8},{8,24},{16,0},{24,16},{1,9},{9,25},{17,1},{25,17},{2,10},{10... | collective-permute-start | bytes 196616 | tf_op jit(solution)/shard_map/ppermute | solution.py:143
  2.9 5.5 %collective-permute-start.1 = (bf16[128,256]{1,0:T(8,128)(2,1)}, bf16[128,256]{1,0:T(8,128)(2,1)S(1)}, u32[]{:S(2)}, u32[]{:S(2)}) collective-permute-start(bf16[128,256]{1,0:T(8,128)(2,1)} %feats_in.1), channel_id=1, source_target_pairs={{0,24},{8,16},{16,8},{24,0},{1,25},{9,17},{17,9},{25,1},{2,26},{10... | collective-permute-start | bytes 196616 | tf_op jit(solution)/shard_map/ppermute | solution.py:143
  4.4 4.5 %collective-permute-start.2 = (bf16[128,256]{1,0:T(8,128)(2,1)}, bf16[128,256]{1,0:T(8,128)(2,1)S(1)}, u32[]{:S(2)}, u32[]{:S(2)}) collective-permute-start(bf16[128,256]{1,0:T(8,128)(2,1)} %feats_in.1), channel_id=1, source_target_pairs={{0,16},{8,0},{16,24},{24,8},{1,17},{9,1},{17,25},{25,9},{2,18},{10... | collective-permute-start | bytes 196616 | tf_op jit(solution)/shard_map/ppermute | solution.py:143
  9.2 1.5 %collective-permute-start.4 = (bf16[2,136,256]{2,1,0:T(8,128)(2,1)S(1)}, bf16[2,136,256]{2,1,0:T(8,128)(2,1)S(1)}, u32[]{:S(2)}, u32[]{:S(2)}) collective-permute-start(bf16[2,136,256]{2,1,0:T(8,128)(2,1)S(1)} %shard_map.69), channel_id=1, source_target_pairs={{0,1},{1,0},{2,3},{3,2},{4,5},{5,4},{6,7},{7,6},{8,9},{9,8},{10,11... | collective-permute-start | bytes 417800 | tf_op jit(solution)/shard_map/ppermute | solution.py:150
  9.6 5.3 %collective-permute-start.3 = (bf16[2,136,256]{2,1,0:T(8,128)(2,1)S(1)}, bf16[2,136,256]{2,1,0:T(8,128)(2,1)S(1)}, u32[]{:S(2)}, u32[]{:S(2)}) collective-permute-start(bf16[2,136,256]{2,1,0:T(8,128)(2,1)S(1)} %shard_map.66), channel_id=1, source_target_pairs={{0,1},{1,0},{2,3},{3,2},{4,5},{5,4},{6,7},{7,6},{8,9},{9,8},{10,11... | collective-permute-start | bytes 417800 | tf_op jit(solution)/shard_map/ppermute | solution.py:150
  10.8 5.8 %collective-permute-start.5 = (bf16[136,256]{1,0:T(8,128)(2,1)S(1)}, bf16[136,256]{1,0:T(8,128)(2,1)S(1)}, u32[]{:S(2)}, u32[]{:S(2)}) collective-permute-start(bf16[136,256]{1,0:T(8,128)(2,1)S(1)} %get-tuple-element.20), channel_id=1, source_target_pairs={{0,2},{1,3},{2,6},{3,7},{4,0},{5,1},{6,4},{7,5},{8,10},{9,11},{10,... | collective-permute-start | bytes 208904 | tf_op jit(solution)/shard_map/ppermute | solution.py:147
  12.4 7.0 %collective-permute-start.6 = (bf16[136,256]{1,0:T(8,128)(2,1)S(1)}, bf16[136,256]{1,0:T(8,128)(2,1)S(1)}, u32[]{:S(2)}, u32[]{:S(2)}) collective-permute-start(bf16[136,256]{1,0:T(8,128)(2,1)S(1)} %get-tuple-element.21), channel_id=1, source_target_pairs={{0,6},{1,7},{2,4},{3,5},{4,2},{5,3},{6,0},{7,1},{8,14},{9,15},{10,... | collective-permute-start | bytes 208904 | tf_op jit(solution)/shard_map/ppermute | solution.py:147
  14.9 4.8 %collective-permute-start.7 = (bf16[136,256]{1,0:T(8,128)(2,1)S(1)}, bf16[136,256]{1,0:T(8,128)(2,1)S(1)}, u32[]{:S(2)}, u32[]{:S(2)}) collective-permute-start(bf16[136,256]{1,0:T(8,128)(2,1)S(1)} %get-tuple-element.22), channel_id=1, source_target_pairs={{0,4},{1,5},{2,0},{3,1},{4,6},{5,7},{6,2},{7,3},{8,12},{9,13},{10,... | collective-permute-start | bytes 208904 | tf_op jit(solution)/shard_map/ppermute | solution.py:147

commit v4 on v3

--- a/solution.py
+++ b/solution.py
@@ -180,7 +180,7 @@
     rows_in = [own_feats] + rows_in
 
     def aggregate(mine, steps):
-        dtype = jnp.float32 if mine else jnp.bfloat16
+        dtype = jnp.float32
         return pl.pallas_call(
             functools.partial(aggregate_kernel, nodes, chips, slots, mine, steps),
             out_shape=jax.ShapeDtypeStruct((len(steps), tile + EXTRA, width), dtype),

time: 20.8 us -> 21 us (level)
  transfers between devices with their start and end apart: 8 -> 8, of which waited for: 3 -> 4; matrix products, arithmetic and copies ran while one was open for 0% -> 0% of each run, Pallas kernels for 17% -> 17%
where the time goes in v4:
time: 21 us; the launch traced here: 20.8 us
  starting transfers between devices  12.3 us (59%)
  Pallas kernels  4.65 us (22%)
  waiting for transfers between devices  3.84 us (18%)
    ppermute x3, starting transfers between devices, over_nodes(): return lax.ppermute(feats, 'node', pairs)  5.92 us
    ppermute x3, starting transfers between devices, over_chips(): return lax.ppermute(array, 'feat', pairs)  5.73 us
    ppermute x3, waiting for transfers between devices, over_chips(): return lax.ppermute(array, 'feat', pairs)  3.33 us
    pallas_call x1, Pallas kernels, body(): pl.pallas_call(prepare_kernel, out_shape=[jax.ShapeDtypeStruct((groups, t...  2.54 us
    pallas_call x4, Pallas kernels, aggregate(): pl.pallas_call(functools.partial(aggregate_kernel, nodes, chips, slots, m...  1.17 us
    pallas_call x1, Pallas kernels, body(): pl.pallas_call(update_kernel, out_shape=jax.ShapeDtypeStruct((tile, width...  0.87 us
    ppermute x2, starting transfers between devices, over_cores(): return lax.ppermute(array, 'feat', [(f, f ^ 1) for f in range(2 * chips)])  0.63 us
  transfers between devices with their start and end apart: 8, of which 4 were waited for; matrix products, arithmetic and copies ran while one was open for 0% of the time, Pallas kernels for 17%

profile of v4, /device:TPU:0, one launch (start us, length us, event | category | flops | bytes accessed | tf_op | source)
XLA Modules:
  0.0 20.8 jit_solution(15701542445513760102)
XLA Ops:
  0.0 2.9 %collective-permute-start = (bf16[128,256]{1,0:T(8,128)(2,1)}, bf16[128,256]{1,0:T(8,128)(2,1)S(1)}, u32[]{:S(2)}, u32[]{:S(2)}) collective-permute-start(bf16[128,256]{1,0:T(8,128)(2,1)} %feats_in.1), channel_id=1, source_target_pairs={{0,8},{8,24},{16,0},{24,16},{1,9},{9,25},{17,1},{25,17},{2,10},{10... | collective-permute-start | bytes 196616 | tf_op jit(solution)/shard_map/ppermute | solution.py:143
  2.9 1.5 %collective-permute-start.1 = (bf16[128,256]{1,0:T(8,128)(2,1)}, bf16[128,256]{1,0:T(8,128)(2,1)S(1)}, u32[]{:S(2)}, u32[]{:S(2)}) collective-permute-start(bf16[128,256]{1,0:T(8,128)(2,1)} %feats_in.1), channel_id=1, source_target_pairs={{0,24},{8,16},{16,8},{24,0},{1,25},{9,17},{17,9},{25,1},{2,26},{10... | collective-permute-start | bytes 196616 | tf_op jit(solution)/shard_map/ppermute | solution.py:143
  4.4 1.5 %collective-permute-start.2 = (bf16[128,256]{1,0:T(8,128)(2,1)}, bf16[128,256]{1,0:T(8,128)(2,1)S(1)}, u32[]{:S(2)}, u32[]{:S(2)}) collective-permute-start(bf16[128,256]{1,0:T(8,128)(2,1)} %feats_in.1), channel_id=1, source_target_pairs={{0,16},{8,0},{16,24},{24,8},{1,17},{9,1},{17,25},{25,9},{2,18},{10... | collective-permute-start | bytes 196616 | tf_op jit(solution)/shard_map/ppermute | solution.py:143
  5.9 2.5 %shard_map.64 = (bf16[8,128,384]{2,1,0:T(8,128)(2,1)S(1)}, f32[8,8,128]{2,1,0:T(8,128)S(1)}, s32[24,128]{1,0:T(8,128)S(1)}, bf16[128,256]{1,0:T(8,128)(2,1)S(1)}...) custom-call(s32[1,8]{1,0:T(1,128)} %bitcast.5, s32[3,8]{1,0:T(4,128)} %bitcast.3, bf16[8,3,128,128]{3,2,1,0:T(8,128)(2,1)} %tiles_in.1, ...), custom_call_target="tpu_custom_call" | custom-call | flops 134217728 | bytes 4194304 | tf_op jit(solution)/shard_map/pallas_call | solution.py:153
  8.5 0.0 collective-permute-done.refs_4_
  8.5 0.0 collective-permute-done.1.refs_5_
  8.5 0.4 %collective-permute-done.2.refs_6_ = bf16[128,256]{1,0:T(8,128)(2,1)S(1)} collective-permute-done((bf16[128,256]{1,0:T(8,128)(2,1)}, bf16[128,256]{1,0:T(8,128)(2,1)S(1)}, u32[]{:S(2)}, u32[]{:S(2)}) %collective-permute-start.2) | collective-permute-done | bytes 65568 | tf_op jit(solution)/shard_map/ppermute | solution.py:143
  8.9 0.3 %shard_map.69 = f32[2,136,256]{2,1,0:T(8,128)S(1)} custom-call(s32[24,128]{1,0:T(8,128)S(1)} %get-tuple-element.15.refs_0_, bf16[8,128,384]{2,1,0:T(8,128)(2,1)S(1)} %get-tuple-element.16.refs_1_, f32[8,8,128]{2,1,0:T(8,128)S(1)} %get-tuple-element.17.refs_2_, bf16[128,256]{1,0:T(8,128)(2,1)S(1)} %get-tuple-element.18.refs_3_.refs_4_, ...), custom_call_target="tpu_custom_call" | custom-call | flops 134217728 | bytes 4194304 | tf_op jit(solution)/shard_map/pallas_call | solution.py:184
  9.2 0.1 collective-permute-start.4
  9.3 0.3 %shard_map.66 = f32[2,136,256]{2,1,0:T(8,128)S(1)} custom-call(s32[24,128]{1,0:T(8,128)S(1)} %get-tuple-element.15.refs_0_, bf16[8,128,384]{2,1,0:T(8,128)(2,1)S(1)} %get-tuple-element.16.refs_1_, f32[8,8,128]{2,1,0:T(8,128)S(1)} %get-tuple-element.17.refs_2_, bf16[128,256]{1,0:T(8,128)(2,1)S(1)} %get-tuple-element.18.refs_3_.refs_4_, ...), custom_call_target="tpu_custom_call" | custom-call | flops 134217728 | bytes 4194304 | tf_op jit(solution)/shard_map/pallas_call | solution.py:184
  9.6 0.6 %collective-permute-start.3 = (f32[2,136,256]{2,1,0:T(8,128)S(1)}, f32[2,136,256]{2,1,0:T(8,128)S(1)}, u32[]{:S(2)}, u32[]{:S(2)}) collective-permute-start(f32[2,136,256]{2,1,0:T(8,128)S(1)} %shard_map.66), channel_id=1, source_target_pairs={{0,1},{1,0},{2,3},{3,2},{4,5},{5,4},{6,7},{7,6},{8,9},{9,8},{10,11... | collective-permute-start | bytes 835592 | tf_op jit(solution)/shard_map/ppermute | solution.py:150
  10.1 0.3 %shard_map.68.mine = f32[2,136,256]{2,1,0:T(8,128)S(1)} custom-call(s32[24,128]{1,0:T(8,128)S(1)} %get-tuple-element.15.refs_0_, bf16[8,128,384]{2,1,0:T(8,128)(2,1)S(1)} %get-tuple-element.16.refs_1_, f32[8,8,128]{2,1,0:T(8,128)S(1)} %get-tuple-element.17.refs_2_, bf16[128,256]{1,0:T(8,128)(2,1)S(1)} %get-tuple-element.18.refs_3_.refs_4_, ...), custom_call_target="tpu_custom_call" | custom-call | flops 134217728 | bytes 4194304 | tf_op jit(solution)/shard_map/pallas_call | solution.py:184
  10.4 0.3 %shard_map.65.mine = f32[2,136,256]{2,1,0:T(8,128)S(1)} custom-call(s32[24,128]{1,0:T(8,128)S(1)} %get-tuple-element.15.refs_0_, bf16[8,128,384]{2,1,0:T(8,128)(2,1)S(1)} %get-tuple-element.16.refs_1_, f32[8,8,128]{2,1,0:T(8,128)S(1)} %get-tuple-element.17.refs_2_, bf16[128,256]{1,0:T(8,128)(2,1)S(1)} %get-tuple-element.18.refs_3_.refs_4_, ...), custom_call_target="tpu_custom_call" | custom-call | flops 134217728 | bytes 4194304 | tf_op jit(solution)/shard_map/pallas_call | solution.py:184
  10.7 0.1 collective-permute-done.4.theirs
  10.9 1.6 %collective-permute-start.5 = (bf16[136,256]{1,0:T(8,128)(2,1)S(1)}, bf16[136,256]{1,0:T(8,128)(2,1)S(1)}, u32[]{:S(2)}, u32[]{:S(2)}) collective-permute-start(bf16[136,256]{1,0:T(8,128)(2,1)S(1)} %get-tuple-element.20), channel_id=1, source_target_pairs={{0,2},{1,3},{2,6},{3,7},{4,0},{5,1},{6,4},{7,5},{8,10},{9,11},{10,... | collective-permute-start | bytes 208904 | tf_op jit(solution)/shard_map/ppermute | solution.py:147
  12.5 2.5 %collective-permute-start.6 = (bf16[136,256]{1,0:T(8,128)(2,1)S(1)}, bf16[136,256]{1,0:T(8,128)(2,1)S(1)}, u32[]{:S(2)}, u32[]{:S(2)}) collective-permute-start(bf16[136,256]{1,0:T(8,128)(2,1)S(1)} %get-tuple-element.21), channel_id=1, source_target_pairs={{0,6},{1,7},{2,4},{3,5},{4,2},{5,3},{6,0},{7,1},{8,14},{9,15},{10,... | collective-permute-start | bytes 208904 | tf_op jit(solution)/shard_map/ppermute | solution.py:147
  15.0 0.0 collective-permute-done.3.theirs
  15.0 1.6 %collective-permute-start.7 = (bf16[136,256]{1,0:T(8,128)(2,1)S(1)}, bf16[136,256]{1,0:T(8,128)(2,1)S(1)}, u32[]{:S(2)}, u32[]{:S(2)}) collective-permute-start(bf16[136,256]{1,0:T(8,128)(2,1)S(1)} %get-tuple-element.22), channel_id=1, source_target_pairs={{0,4},{1,5},{2,0},{3,1},{4,6},{5,7},{6,2},{7,3},{8,12},{9,13},{10,... | collective-permute-start | bytes 208904 | tf_op jit(solution)/shard_map/ppermute | solution.py:147
  16.6 0.0 collective-permute-done.5.refs_1_
  16.6 2.8 %collective-permute-done.6.refs_2_ = bf16[136,256]{1,0:T(8,128)(2,1)S(1)} collective-permute-done((bf16[136,256]{1,0:T(8,128)(2,1)S(1)}, bf16[136,256]{1,0:T(8,128)(2,1)S(1)}, u32[]{:S(2)}, u32[]{:S(2)}) %collective-permute-start.6) | collective-permute-done | bytes 69664 | tf_op jit(solution)/shard_map/ppermute | solution.py:147
  19.5 0.5 %collective-permute-done.7.refs_3_ = bf16[136,256]{1,0:T(8,128)(2,1)S(1)} collective-permute-done((bf16[136,256]{1,0:T(8,128)(2,1)S(1)}, bf16[136,256]{1,0:T(8,128)(2,1)S(1)}, u32[]{:S(2)}, u32[]{:S(2)}) %collective-permute-start.7) | collective-permute-done | bytes 69664 | tf_op jit(solution)/shard_map/ppermute | solution.py:147
  20.0 0.9 %shard_map.71 = bf16[128,256]{1,0:T(8,128)(2,1)} custom-call(f32[136,256]{1,0:T(8,128)S(1)} %get-tuple-element.19.refs_0_, bf16[136,256]{1,0:T(8,128)(2,1)S(1)} %collective-permute-done.5.refs_1_, bf16[136,256]{1,0:T(8,128)(2,1)S(1)} %collective-permute-done.6.refs_2_, bf16[136,256]{1,0:T(8,128)(2,1)S(1)} %collective-permute-done.7.refs_3_, ...), custom_call_target="tpu_custom_call" | custom-call | tf_op jit(solution)/shard_map/pallas_call | solution.py:210
  (2 shorter events, 0.1 us)
Async XLA Ops:
  0.0 8.5 %collective-permute-start = (bf16[128,256]{1,0:T(8,128)(2,1)}, bf16[128,256]{1,0:T(8,128)(2,1)S(1)}, u32[]{:S(2)}, u32[]{:S(2)}) collective-permute-start(bf16[128,256]{1,0:T(8,128)(2,1)} %feats_in.1), channel_id=1, source_target_pairs={{0,8},{8,24},{16,0},{24,16},{1,9},{9,25},{17,1},{25,17},{2,10},{10... | collective-permute-start | bytes 196616 | tf_op jit(solution)/shard_map/ppermute | solution.py:143
  2.9 5.5 %collective-permute-start.1 = (bf16[128,256]{1,0:T(8,128)(2,1)}, bf16[128,256]{1,0:T(8,128)(2,1)S(1)}, u32[]{:S(2)}, u32[]{:S(2)}) collective-permute-start(bf16[128,256]{1,0:T(8,128)(2,1)} %feats_in.1), channel_id=1, source_target_pairs={{0,24},{8,16},{16,8},{24,0},{1,25},{9,17},{17,9},{25,1},{2,26},{10... | collective-permute-start | bytes 196616 | tf_op jit(solution)/shard_map/ppermute | solution.py:143
  4.4 4.5 %collective-permute-start.2 = (bf16[128,256]{1,0:T(8,128)(2,1)}, bf16[128,256]{1,0:T(8,128)(2,1)S(1)}, u32[]{:S(2)}, u32[]{:S(2)}) collective-permute-start(bf16[128,256]{1,0:T(8,128)(2,1)} %feats_in.1), channel_id=1, source_target_pairs={{0,16},{8,0},{16,24},{24,8},{1,17},{9,1},{17,25},{25,9},{2,18},{10... | collective-permute-start | bytes 196616 | tf_op jit(solution)/shard_map/ppermute | solution.py:143
  9.2 1.6 %collective-permute-start.4 = (f32[2,136,256]{2,1,0:T(8,128)S(1)}, f32[2,136,256]{2,1,0:T(8,128)S(1)}, u32[]{:S(2)}, u32[]{:S(2)}) collective-permute-start(f32[2,136,256]{2,1,0:T(8,128)S(1)} %shard_map.69), channel_id=1, source_target_pairs={{0,1},{1,0},{2,3},{3,2},{4,5},{5,4},{6,7},{7,6},{8,9},{9,8},{10,11... | collective-permute-start | bytes 835592 | tf_op jit(solution)/shard_map/ppermute | solution.py:150
  9.6 5.4 %collective-permute-start.3 = (f32[2,136,256]{2,1,0:T(8,128)S(1)}, f32[2,136,256]{2,1,0:T(8,128)S(1)}, u32[]{:S(2)}, u32[]{:S(2)}) collective-permute-start(f32[2,136,256]{2,1,0:T(8,128)S(1)} %shard_map.66), channel_id=1, source_target_pairs={{0,1},{1,0},{2,3},{3,2},{4,5},{5,4},{6,7},{7,6},{8,9},{9,8},{10,11... | collective-permute-start | bytes 835592 | tf_op jit(solution)/shard_map/ppermute | solution.py:150
  10.9 5.8 %collective-permute-start.5 = (bf16[136,256]{1,0:T(8,128)(2,1)S(1)}, bf16[136,256]{1,0:T(8,128)(2,1)S(1)}, u32[]{:S(2)}, u32[]{:S(2)}) collective-permute-start(bf16[136,256]{1,0:T(8,128)(2,1)S(1)} %get-tuple-element.20), channel_id=1, source_target_pairs={{0,2},{1,3},{2,6},{3,7},{4,0},{5,1},{6,4},{7,5},{8,10},{9,11},{10,... | collective-permute-start | bytes 208904 | tf_op jit(solution)/shard_map/ppermute | solution.py:147
  12.5 7.0 %collective-permute-start.6 = (bf16[136,256]{1,0:T(8,128)(2,1)S(1)}, bf16[136,256]{1,0:T(8,128)(2,1)S(1)}, u32[]{:S(2)}, u32[]{:S(2)}) collective-permute-start(bf16[136,256]{1,0:T(8,128)(2,1)S(1)} %get-tuple-element.21), channel_id=1, source_target_pairs={{0,6},{1,7},{2,4},{3,5},{4,2},{5,3},{6,0},{7,1},{8,14},{9,15},{10,... | collective-permute-start | bytes 208904 | tf_op jit(solution)/shard_map/ppermute | solution.py:147
  15.0 5.0 %collective-permute-start.7 = (bf16[136,256]{1,0:T(8,128)(2,1)S(1)}, bf16[136,256]{1,0:T(8,128)(2,1)S(1)}, u32[]{:S(2)}, u32[]{:S(2)}) collective-permute-start(bf16[136,256]{1,0:T(8,128)(2,1)S(1)} %get-tuple-element.22), channel_id=1, source_target_pairs={{0,4},{1,5},{2,0},{3,1},{4,6},{5,7},{6,2},{7,3},{8,12},{9,13},{10,... | collective-permute-start | bytes 208904 | tf_op jit(solution)/shard_map/ppermute | solution.py:147

commit v5 on v3

--- a/solution.py
+++ b/solution.py
@@ -94,7 +94,7 @@
 def aggregate_kernel(nodes, chips, slots, mine, steps, *refs):
     chosen, adjacency, degree = refs[:3]
     feats_in = refs[3 : 3 + nodes]
-    out, rows = refs[3 + nodes :]
+    out, rows = refs[-2:]
     node = lax.axis_index("node")
     tile = feats_in[0].shape[0]
     for step in range(nodes):
@@ -108,28 +108,35 @@
         out[index, tile:] = split_rows(degree[place]).astype(out.dtype)
 
 
-def merge_kernel(mine, theirs, *outs):
+def merge_kernel(first, count, mine, theirs, *outs):
+    outs = outs[-count:]
     tile = mine.shape[1] - EXTRA
     for index, out in enumerate(outs):
-        total = mine[index, :tile] + theirs[index, :tile].astype(jnp.float32)
-        degree = split_rows(join_rows(mine[index, tile:]) + join_rows(theirs[index, tile:]))
+        total = mine[first + index, :tile] + theirs[index, :tile].astype(jnp.float32)
+        degree = split_rows(join_rows(mine[first + index, tile:]) + join_rows(theirs[index, tile:]))
         out[:tile] = total.astype(out.dtype)
         out[tile:] = degree.astype(out.dtype)
 
 
-def update_kernel(*refs):
-    own, *parts, feats, weight, bias, out = refs
+def gather_kernel(own, *refs):
+    *parts, feats, out = refs
     tile = feats.shape[0]
     total = own[...]
     for part in parts:
         total = total + part[...].astype(jnp.float32)
+    out[:tile] = total[:tile] + feats[...].astype(jnp.float32)
+    out[tile:] = total[tile:]
+
+
+def update_kernel(earlier, last, feats, weight, bias, out):
+    tile = feats.shape[0]
+    total = earlier[...] + last[...].astype(jnp.float32)
     degree = join_rows(total[tile:])[:1]
     scale = jnp.transpose(jnp.broadcast_to(lax.rsqrt(degree + 1.0), (tile, tile)))
     scale = jnp.concatenate([scale] * (feats.shape[1] // tile), axis=1)
-    rows = feats[...].astype(jnp.float32)
-    normed = ((total[:tile] + rows) * scale).astype(jnp.bfloat16)
+    normed = (total[:tile] * scale).astype(jnp.bfloat16)
     hidden = jnp.dot(normed, weight[...], preferred_element_type=jnp.float32) + bias[...]
-    out[...] = (rows + jnp.maximum(hidden, 0.0)).astype(jnp.bfloat16)
+    out[...] = (feats[...].astype(jnp.float32) + jnp.maximum(hidden, 0.0)).astype(jnp.bfloat16)
 
 
 def body(mesh, feats, tile_values, source_group, live_slots, proj_weight, proj_bias):
@@ -179,41 +186,52 @@
     )
     rows_in = [own_feats] + rows_in
 
-    def aggregate(mine, steps):
+    def aggregate(mine, steps, *after):
         dtype = jnp.float32 if mine else jnp.bfloat16
         return pl.pallas_call(
             functools.partial(aggregate_kernel, nodes, chips, slots, mine, steps),
             out_shape=jax.ShapeDtypeStruct((len(steps), tile + EXTRA, width), dtype),
-            in_specs=[VMEM] * (3 + nodes),
+            in_specs=[VMEM] * (3 + nodes + len(after)),
             out_specs=VMEM,
             scratch_shapes=[pltpu.VMEM((nodes, tile, width), jnp.bfloat16)],
             compiler_params=PARAMS,
             cost_estimate=pl.CostEstimate(flops=1 << 27, bytes_accessed=1 << 22, transcendentals=0),
-        )(chosen, adjacency, degree, *rows_in)
-
-    def merge(mine, theirs, dtypes):
+        )(chosen, adjacency, degree, *rows_in, *after)
+
+    def merge(first, mine, theirs, dtypes, *after):
         return pl.pallas_call(
-            merge_kernel,
+            functools.partial(merge_kernel, first, len(dtypes)),
             out_shape=[jax.ShapeDtypeStruct((tile + EXTRA, width), dtype) for dtype in dtypes],
-            in_specs=[VMEM] * 2,
+            in_specs=[VMEM] * (2 + len(after)),
             out_specs=[VMEM] * len(dtypes),
             compiler_params=PARAMS,
-        )(mine, theirs)
+        )(mine, theirs, *after)
 
     cut = min(chips, FIRST + 1)
     far, near = list(range(1, cut)), list(range(cut, chips)) + [0]
-    theirs_far = over_cores(aggregate(0, far))
-    theirs_near = over_cores(aggregate(0, near))
-    parts = merge(aggregate(1, far), theirs_far, [jnp.bfloat16] * len(far))
-    *rest, own = merge(aggregate(1, near), theirs_near, [jnp.bfloat16] * (len(near) - 1) + [jnp.float32])
+    first = aggregate(0, far)
+    mine = aggregate(1, far + near, first)
+    second = aggregate(0, near, mine)
+    parts = merge(0, mine, over_cores(first), [jnp.bfloat16] * len(far))
+    *rest, own = merge(
+        len(far), mine, over_cores(second), [jnp.bfloat16] * (len(near) - 1) + [jnp.float32]
+    )
     parts = [over_chips(part, step) for step, part in enumerate([*parts, *rest], 1)]
+    *parts, last = parts
+    earlier = pl.pallas_call(
+        gather_kernel,
+        out_shape=jax.ShapeDtypeStruct((tile + EXTRA, width), jnp.float32),
+        in_specs=[VMEM] * (len(parts) + 2),
+        out_specs=VMEM,
+        compiler_params=PARAMS,
+    )(own, *parts, own_feats)
     return pl.pallas_call(
         update_kernel,
         out_shape=jax.ShapeDtypeStruct((tile, width), jnp.bfloat16),
-        in_specs=[VMEM] * (chips + 3),
+        in_specs=[VMEM] * 5,
         out_specs=VMEM,
         compiler_params=PARAMS,
-    )(own, *parts, own_feats, weight, bias)
+    )(earlier, last, own_feats, weight, bias)
 
 
 def solution(mesh):

time: 20.8 us -> 20.8 us (level)
  starting transfers between devices: 12.3 us -> 12.6 us
  waiting for transfers between devices: 3.64 us -> 3.41 us
    ppermute x3, waiting for transfers between devices: 0.42 us -> 0.01 us  [over_nodes(): return lax.ppermute(feats, 'node', pairs)]
    ppermute x3, starting transfers between devices: 5.73 us -> 6.07 us  [over_chips(): return lax.ppermute(array, 'feat', pairs)]
    pallas_call x4 -> x3, Pallas kernels: 1.17 us -> 0.97 us  [aggregate(): pl.pallas_call(functools.partial(aggregate_kernel, nodes, chips, slots, m...]
  transfers between devices with their start and end apart: 8 -> 8, of which waited for: 3 -> 3; matrix products, arithmetic and copies ran while one was open for 0% -> 0% of each run, Pallas kernels for 17% -> 16%
where the time goes in v5:
time: 20.8 us; the launch traced here: 20.6 us
  starting transfers between devices  12.6 us (61%)
  Pallas kernels  4.5 us (22%)
  waiting for transfers between devices  3.41 us (16%)
    ppermute x3, starting transfers between devices, over_chips(): return lax.ppermute(array, 'feat', pairs)  6.07 us
    ppermute x3, starting transfers between devices, over_nodes(): return lax.ppermute(feats, 'node', pairs)  5.92 us
    ppermute x3, waiting for transfers between devices, over_chips(): return lax.ppermute(array, 'feat', pairs)  3.3 us
    pallas_call x1, Pallas kernels, body(): pl.pallas_call(prepare_kernel, out_shape=[jax.ShapeDtypeStruct((groups, t...  2.54 us
    pallas_call x3, Pallas kernels, aggregate(): pl.pallas_call(functools.partial(aggregate_kernel, nodes, chips, slots, m...  0.97 us
    pallas_call x1, Pallas kernels, body(): pl.pallas_call(update_kernel, out_shape=jax.ShapeDtypeStruct((tile, width...  0.87 us
    ppermute x2, starting transfers between devices, over_cores(): return lax.ppermute(array, 'feat', [(f, f ^ 1) for f in range(2 * chips)])  0.63 us
  transfers between devices with their start and end apart: 8, of which 3 were waited for; matrix products, arithmetic and copies ran while one was open for 0% of the time, Pallas kernels for 16%

profile of v5, /device:TPU:0, one launch (start us, length us, event | category | flops | bytes accessed | tf_op | source)
XLA Modules:
  0.0 20.6 jit_solution(6679378327002133492)
XLA Ops:
  0.0 2.9 %collective-permute-start = (bf16[128,256]{1,0:T(8,128)(2,1)}, bf16[128,256]{1,0:T(8,128)(2,1)S(1)}, u32[]{:S(2)}, u32[]{:S(2)}) collective-permute-start(bf16[128,256]{1,0:T(8,128)(2,1)} %feats_in.1), channel_id=1, source_target_pairs={{0,8},{8,24},{16,0},{24,16},{1,9},{9,25},{17,1},{25,17},{2,10},{10... | collective-permute-start | bytes 196616 | tf_op jit(solution)/shard_map/ppermute | solution.py:150
  2.9 0.0 collective-permute-start.2
  3.0 3.0 %collective-permute-start.1 = (bf16[128,256]{1,0:T(8,128)(2,1)}, bf16[128,256]{1,0:T(8,128)(2,1)S(1)}, u32[]{:S(2)}, u32[]{:S(2)}) collective-permute-start(bf16[128,256]{1,0:T(8,128)(2,1)} %feats_in.1), channel_id=1, source_target_pairs={{0,24},{8,16},{16,8},{24,0},{1,25},{9,17},{17,9},{25,1},{2,26},{10... | collective-permute-start | bytes 196616 | tf_op jit(solution)/shard_map/ppermute | solution.py:150
  5.9 2.5 %shard_map.64 = (bf16[8,128,384]{2,1,0:T(8,128)(2,1)S(1)}, f32[8,8,128]{2,1,0:T(8,128)S(1)}, s32[24,128]{1,0:T(8,128)S(1)}, bf16[128,256]{1,0:T(8,128)(2,1)S(1)}...) custom-call(s32[1,8]{1,0:T(1,128)} %bitcast.5, s32[3,8]{1,0:T(4,128)} %bitcast.3, bf16[8,3,128,128]{3,2,1,0:T(8,128)(2,1)} %tiles_in.1, ...), custom_call_target="tpu_custom_call" | custom-call | flops 134217728 | bytes 4194304 | tf_op jit(solution)/shard_map/pallas_call | solution.py:160
  8.5 0.0 collective-permute-done.refs_4_
  8.5 0.0 collective-permute-done.2.refs_6_
  8.5 0.0 collective-permute-done.1.refs_5_
  8.5 0.3 %shard_map.65.refs_7_ = bf16[2,136,256]{2,1,0:T(8,128)(2,1)S(1)} custom-call(s32[24,128]{1,0:T(8,128)S(1)} %get-tuple-element.15.refs_0_, bf16[8,128,384]{2,1,0:T(8,128)(2,1)S(1)} %get-tuple-element.16.refs_1_, f32[8,8,128]{2,1,0:T(8,128)S(1)} %get-tuple-element.17.refs_2_, bf16[128,256]{1,0:T(8,128)(2,1)S(1)} %get-tuple-element.18.refs_3_.refs_2_.feats, ...), custom_call_target="tpu_custom_call" | custom-call | flops 134217728 | bytes 4194304 | tf_op jit(solution)/shard_map/pallas_call | solution.py:191
  8.8 0.1 collective-permute-start.4
  8.9 0.4 %shard_map.66.refs_7_.mine = f32[4,136,256]{2,1,0:T(8,128)S(1)} custom-call(s32[24,128]{1,0:T(8,128)S(1)} %get-tuple-element.15.refs_0_, bf16[8,128,384]{2,1,0:T(8,128)(2,1)S(1)} %get-tuple-element.16.refs_1_, f32[8,8,128]{2,1,0:T(8,128)S(1)} %get-tuple-element.17.refs_2_, bf16[128,256]{1,0:T(8,128)(2,1)S(1)} %get-tuple-element.18.refs_3_.refs_2_.feats, ...), custom_call_target="tpu_custom_call" | custom-call | flops 134217728 | bytes 4194304 | tf_op jit(solution)/shard_map/pallas_call | solution.py:191
  9.3 0.3 %shard_map.67 = bf16[2,136,256]{2,1,0:T(8,128)(2,1)S(1)} custom-call(s32[24,128]{1,0:T(8,128)S(1)} %get-tuple-element.15.refs_0_, bf16[8,128,384]{2,1,0:T(8,128)(2,1)S(1)} %get-tuple-element.16.refs_1_, f32[8,8,128]{2,1,0:T(8,128)S(1)} %get-tuple-element.17.refs_2_, bf16[128,256]{1,0:T(8,128)(2,1)S(1)} %get-tuple-element.18.refs_3_.refs_2_.feats, ...), custom_call_target="tpu_custom_call" | custom-call | flops 134217728 | bytes 4194304 | tf_op jit(solution)/shard_map/pallas_call | solution.py:191
  9.6 0.6 %collective-permute-start.3 = (bf16[2,136,256]{2,1,0:T(8,128)(2,1)S(1)}, bf16[2,136,256]{2,1,0:T(8,128)(2,1)S(1)}, u32[]{:S(2)}, u32[]{:S(2)}) collective-permute-start(bf16[2,136,256]{2,1,0:T(8,128)(2,1)S(1)} %shard_map.67), channel_id=1, source_target_pairs={{0,1},{1,0},{2,3},{3,2},{4,5},{5,4},{6,7},{7,6},{8,9},{9,8},{10,11... | collective-permute-start | bytes 417800 | tf_op jit(solution)/shard_map/ppermute | solution.py:157
  10.1 0.1 collective-permute-done.4.theirs
  10.3 2.0 %collective-permute-start.5 = (bf16[136,256]{1,0:T(8,128)(2,1)S(1)}, bf16[136,256]{1,0:T(8,128)(2,1)S(1)}, u32[]{:S(2)}, u32[]{:S(2)}) collective-permute-start(bf16[136,256]{1,0:T(8,128)(2,1)S(1)} %get-tuple-element.20), channel_id=1, source_target_pairs={{0,2},{1,3},{2,6},{3,7},{4,0},{5,1},{6,4},{7,5},{8,10},{9,11},{10,... | collective-permute-start | bytes 208904 | tf_op jit(solution)/shard_map/ppermute | solution.py:154
  12.2 2.5 %collective-permute-start.6 = (bf16[136,256]{1,0:T(8,128)(2,1)S(1)}, bf16[136,256]{1,0:T(8,128)(2,1)S(1)}, u32[]{:S(2)}, u32[]{:S(2)}) collective-permute-start(bf16[136,256]{1,0:T(8,128)(2,1)S(1)} %get-tuple-element.21), channel_id=1, source_target_pairs={{0,6},{1,7},{2,4},{3,5},{4,2},{5,3},{6,0},{7,1},{8,14},{9,15},{10,... | collective-permute-start | bytes 208904 | tf_op jit(solution)/shard_map/ppermute | solution.py:154
  14.7 0.0 collective-permute-done.3.theirs
  14.8 1.6 %collective-permute-start.7 = (bf16[136,256]{1,0:T(8,128)(2,1)S(1)}, bf16[136,256]{1,0:T(8,128)(2,1)S(1)}, u32[]{:S(2)}, u32[]{:S(2)}) collective-permute-start(bf16[136,256]{1,0:T(8,128)(2,1)S(1)} %get-tuple-element.22), channel_id=1, source_target_pairs={{0,4},{1,5},{2,0},{3,1},{4,6},{5,7},{6,2},{7,3},{8,12},{9,13},{10,... | collective-permute-start | bytes 208904 | tf_op jit(solution)/shard_map/ppermute | solution.py:154
  16.4 0.0 collective-permute-done.5.refs_0_
  16.4 2.8 %collective-permute-done.6.refs_1_ = bf16[136,256]{1,0:T(8,128)(2,1)S(1)} collective-permute-done((bf16[136,256]{1,0:T(8,128)(2,1)S(1)}, bf16[136,256]{1,0:T(8,128)(2,1)S(1)}, u32[]{:S(2)}, u32[]{:S(2)}) %collective-permute-start.6) | collective-permute-done | bytes 69664 | tf_op jit(solution)/shard_map/ppermute | solution.py:154
  19.2 0.5 %collective-permute-done.7.last = bf16[136,256]{1,0:T(8,128)(2,1)S(1)} collective-permute-done((bf16[136,256]{1,0:T(8,128)(2,1)S(1)}, bf16[136,256]{1,0:T(8,128)(2,1)S(1)}, u32[]{:S(2)}, u32[]{:S(2)}) %collective-permute-start.7) | collective-permute-done | bytes 69664 | tf_op jit(solution)/shard_map/ppermute | solution.py:154
  19.7 0.9 %shard_map.71 = bf16[128,256]{1,0:T(8,128)(2,1)} custom-call(f32[136,256]{1,0:T(8,128)S(1)} %shard_map.70.earlier, bf16[136,256]{1,0:T(8,128)(2,1)S(1)} %collective-permute-done.7.last, bf16[128,256]{1,0:T(8,128)(2,1)S(1)} %get-tuple-element.18.refs_3_.refs_2_.feats, bf16[256,256]{1,0:T(8,128)(2,1)S(1)} %get-tuple-element.23.weight, ...), custom_call_target="tpu_custom_call" | custom-call | tf_op jit(solution)/shard_map/pallas_call | solution.py:228
  (3 shorter events, 0.1 us)
Async XLA Ops:
  0.0 8.5 %collective-permute-start = (bf16[128,256]{1,0:T(8,128)(2,1)}, bf16[128,256]{1,0:T(8,128)(2,1)S(1)}, u32[]{:S(2)}, u32[]{:S(2)}) collective-permute-start(bf16[128,256]{1,0:T(8,128)(2,1)} %feats_in.1), channel_id=1, source_target_pairs={{0,8},{8,24},{16,0},{24,16},{1,9},{9,25},{17,1},{25,17},{2,10},{10... | collective-permute-start | bytes 196616 | tf_op jit(solution)/shard_map/ppermute | solution.py:150
  2.9 5.5 %collective-permute-start.2 = (bf16[128,256]{1,0:T(8,128)(2,1)}, bf16[128,256]{1,0:T(8,128)(2,1)S(1)}, u32[]{:S(2)}, u32[]{:S(2)}) collective-permute-start(bf16[128,256]{1,0:T(8,128)(2,1)} %feats_in.1), channel_id=1, source_target_pairs={{0,16},{8,0},{16,24},{24,8},{1,17},{9,1},{17,25},{25,9},{2,18},{10... | collective-permute-start | bytes 196616 | tf_op jit(solution)/shard_map/ppermute | solution.py:150
  3.0 5.5 %collective-permute-start.1 = (bf16[128,256]{1,0:T(8,128)(2,1)}, bf16[128,256]{1,0:T(8,128)(2,1)S(1)}, u32[]{:S(2)}, u32[]{:S(2)}) collective-permute-start(bf16[128,256]{1,0:T(8,128)(2,1)} %feats_in.1), channel_id=1, source_target_pairs={{0,24},{8,16},{16,8},{24,0},{1,25},{9,17},{17,9},{25,1},{2,26},{10... | collective-permute-start | bytes 196616 | tf_op jit(solution)/shard_map/ppermute | solution.py:150
  8.8 1.4 %collective-permute-start.4 = (bf16[2,136,256]{2,1,0:T(8,128)(2,1)S(1)}, bf16[2,136,256]{2,1,0:T(8,128)(2,1)S(1)}, u32[]{:S(2)}, u32[]{:S(2)}) collective-permute-start(bf16[2,136,256]{2,1,0:T(8,128)(2,1)S(1)} %shard_map.65.refs_7_), channel_id=1, source_target_pairs={{0,1},{1,0},{2,3},{3,2},{4,5},{5,4},{6,7},{7,6},{8,9},{9,8},{10,11... | collective-permute-start | bytes 417800 | tf_op jit(solution)/shard_map/ppermute | solution.py:157
  9.6 5.1 %collective-permute-start.3 = (bf16[2,136,256]{2,1,0:T(8,128)(2,1)S(1)}, bf16[2,136,256]{2,1,0:T(8,128)(2,1)S(1)}, u32[]{:S(2)}, u32[]{:S(2)}) collective-permute-start(bf16[2,136,256]{2,1,0:T(8,128)(2,1)S(1)} %shard_map.67), channel_id=1, source_target_pairs={{0,1},{1,0},{2,3},{3,2},{4,5},{5,4},{6,7},{7,6},{8,9},{9,8},{10,11... | collective-permute-start | bytes 417800 | tf_op jit(solution)/shard_map/ppermute | solution.py:157
  10.3 6.1 %collective-permute-start.5 = (bf16[136,256]{1,0:T(8,128)(2,1)S(1)}, bf16[136,256]{1,0:T(8,128)(2,1)S(1)}, u32[]{:S(2)}, u32[]{:S(2)}) collective-permute-start(bf16[136,256]{1,0:T(8,128)(2,1)S(1)} %get-tuple-element.20), channel_id=1, source_target_pairs={{0,2},{1,3},{2,6},{3,7},{4,0},{5,1},{6,4},{7,5},{8,10},{9,11},{10,... | collective-permute-start | bytes 208904 | tf_op jit(solution)/shard_map/ppermute | solution.py:154
  12.2 7.0 %collective-permute-start.6 = (bf16[136,256]{1,0:T(8,128)(2,1)S(1)}, bf16[136,256]{1,0:T(8,128)(2,1)S(1)}, u32[]{:S(2)}, u32[]{:S(2)}) collective-permute-start(bf16[136,256]{1,0:T(8,128)(2,1)S(1)} %get-tuple-element.21), channel_id=1, source_target_pairs={{0,6},{1,7},{2,4},{3,5},{4,2},{5,3},{6,0},{7,1},{8,14},{9,15},{10,... | collective-permute-start | bytes 208904 | tf_op jit(solution)/shard_map/ppermute | solution.py:154
  14.8 5.0 %collective-permute-start.7 = (bf16[136,256]{1,0:T(8,128)(2,1)S(1)}, bf16[136,256]{1,0:T(8,128)(2,1)S(1)}, u32[]{:S(2)}, u32[]{:S(2)}) collective-permute-start(bf16[136,256]{1,0:T(8,128)(2,1)S(1)} %get-tuple-element.22), channel_id=1, source_target_pairs={{0,4},{1,5},{2,0},{3,1},{4,6},{5,7},{6,2},{7,3},{8,12},{9,13},{10,... | collective-permute-start | bytes 208904 | tf_op jit(solution)/shard_map/ppermute | solution.py:154

commit v6 on v5

--- a/solution.py
+++ b/solution.py
@@ -187,10 +187,9 @@
     rows_in = [own_feats] + rows_in
 
     def aggregate(mine, steps, *after):
-        dtype = jnp.float32 if mine else jnp.bfloat16
         return pl.pallas_call(
             functools.partial(aggregate_kernel, nodes, chips, slots, mine, steps),
-            out_shape=jax.ShapeDtypeStruct((len(steps), tile + EXTRA, width), dtype),
+            out_shape=jax.ShapeDtypeStruct((len(steps), tile + EXTRA, width), jnp.float32),
             in_specs=[VMEM] * (3 + nodes + len(after)),
             out_specs=VMEM,
             scratch_shapes=[pltpu.VMEM((nodes, tile, width), jnp.bfloat16)],

time: 20.8 us -> 20.9 us (level)
  no operation moved by 1% of the time
where the time goes in v6:
time: 20.9 us; the launch traced here: 20.8 us
  starting transfers between devices  12.6 us (60%)
  Pallas kernels  4.48 us (21%)
  waiting for transfers between devices  3.6 us (17%)
    ppermute x3, starting transfers between devices, over_chips(): return lax.ppermute(array, 'feat', pairs)  6.07 us
    ppermute x3, starting transfers between devices, over_nodes(): return lax.ppermute(feats, 'node', pairs)  5.92 us
    ppermute x3, waiting for transfers between devices, over_chips(): return lax.ppermute(array, 'feat', pairs)  3.29 us
    pallas_call x1, Pallas kernels, body(): pl.pallas_call(prepare_kernel, out_shape=[jax.ShapeDtypeStruct((groups, t...  2.54 us
    pallas_call x3, Pallas kernels, aggregate(): pl.pallas_call(functools.partial(aggregate_kernel, nodes, chips, slots, m...  0.97 us
    pallas_call x1, Pallas kernels, body(): pl.pallas_call(update_kernel, out_shape=jax.ShapeDtypeStruct((tile, width...  0.87 us
    ppermute x2, starting transfers between devices, over_cores(): return lax.ppermute(array, 'feat', [(f, f ^ 1) for f in range(2 * chips)])  0.63 us
  transfers between devices with their start and end apart: 8, of which 3 were waited for; matrix products, arithmetic and copies ran while one was open for 0% of the time, Pallas kernels for 16%

profile of v6, /device:TPU:0, one launch (start us, length us, event | category | flops | bytes accessed | tf_op | source)
XLA Modules:
  0.0 20.8 jit_solution(11827659532181193551)
XLA Ops:
  0.0 2.9 %collective-permute-start = (bf16[128,256]{1,0:T(8,128)(2,1)}, bf16[128,256]{1,0:T(8,128)(2,1)S(1)}, u32[]{:S(2)}, u32[]{:S(2)}) collective-permute-start(bf16[128,256]{1,0:T(8,128)(2,1)} %feats_in.1), channel_id=1, source_target_pairs={{0,8},{8,24},{16,0},{24,16},{1,9},{9,25},{17,1},{25,17},{2,10},{10... | collective-permute-start | bytes 196616 | tf_op jit(solution)/shard_map/ppermute | solution.py:150
  2.9 0.0 collective-permute-start.2
  3.0 3.0 %collective-permute-start.1 = (bf16[128,256]{1,0:T(8,128)(2,1)}, bf16[128,256]{1,0:T(8,128)(2,1)S(1)}, u32[]{:S(2)}, u32[]{:S(2)}) collective-permute-start(bf16[128,256]{1,0:T(8,128)(2,1)} %feats_in.1), channel_id=1, source_target_pairs={{0,24},{8,16},{16,8},{24,0},{1,25},{9,17},{17,9},{25,1},{2,26},{10... | collective-permute-start | bytes 196616 | tf_op jit(solution)/shard_map/ppermute | solution.py:150
  5.9 2.5 %shard_map.64 = (bf16[8,128,384]{2,1,0:T(8,128)(2,1)S(1)}, f32[8,8,128]{2,1,0:T(8,128)S(1)}, s32[24,128]{1,0:T(8,128)S(1)}, bf16[128,256]{1,0:T(8,128)(2,1)S(1)}...) custom-call(s32[1,8]{1,0:T(1,128)} %bitcast.5, s32[3,8]{1,0:T(4,128)} %bitcast.3, bf16[8,3,128,128]{3,2,1,0:T(8,128)(2,1)} %tiles_in.1, ...), custom_call_target="tpu_custom_call" | custom-call | flops 134217728 | bytes 4194304 | tf_op jit(solution)/shard_map/pallas_call | solution.py:160
  8.5 0.0 collective-permute-done.refs_4_
  8.5 0.0 collective-permute-done.2.refs_6_
  8.5 0.0 collective-permute-done.1.refs_5_
  8.5 0.3 %shard_map.65.refs_7_ = f32[2,136,256]{2,1,0:T(8,128)S(1)} custom-call(s32[24,128]{1,0:T(8,128)S(1)} %get-tuple-element.15.refs_0_, bf16[8,128,384]{2,1,0:T(8,128)(2,1)S(1)} %get-tuple-element.16.refs_1_, f32[8,8,128]{2,1,0:T(8,128)S(1)} %get-tuple-element.17.refs_2_, bf16[128,256]{1,0:T(8,128)(2,1)S(1)} %get-tuple-element.18.refs_3_.refs_2_.feats, ...), custom_call_target="tpu_custom_call" | custom-call | flops 134217728 | bytes 4194304 | tf_op jit(solution)/shard_map/pallas_call | solution.py:190
  8.8 0.1 collective-permute-start.4
  8.9 0.4 %shard_map.66.refs_7_.mine = f32[4,136,256]{2,1,0:T(8,128)S(1)} custom-call(s32[24,128]{1,0:T(8,128)S(1)} %get-tuple-element.15.refs_0_, bf16[8,128,384]{2,1,0:T(8,128)(2,1)S(1)} %get-tuple-element.16.refs_1_, f32[8,8,128]{2,1,0:T(8,128)S(1)} %get-tuple-element.17.refs_2_, bf16[128,256]{1,0:T(8,128)(2,1)S(1)} %get-tuple-element.18.refs_3_.refs_2_.feats, ...), custom_call_target="tpu_custom_call" | custom-call | flops 134217728 | bytes 4194304 | tf_op jit(solution)/shard_map/pallas_call | solution.py:190
  9.3 0.3 %shard_map.67 = f32[2,136,256]{2,1,0:T(8,128)S(1)} custom-call(s32[24,128]{1,0:T(8,128)S(1)} %get-tuple-element.15.refs_0_, bf16[8,128,384]{2,1,0:T(8,128)(2,1)S(1)} %get-tuple-element.16.refs_1_, f32[8,8,128]{2,1,0:T(8,128)S(1)} %get-tuple-element.17.refs_2_, bf16[128,256]{1,0:T(8,128)(2,1)S(1)} %get-tuple-element.18.refs_3_.refs_2_.feats, ...), custom_call_target="tpu_custom_call" | custom-call | flops 134217728 | bytes 4194304 | tf_op jit(solution)/shard_map/pallas_call | solution.py:190
  9.6 0.6 %collective-permute-start.3 = (f32[2,136,256]{2,1,0:T(8,128)S(1)}, f32[2,136,256]{2,1,0:T(8,128)S(1)}, u32[]{:S(2)}, u32[]{:S(2)}) collective-permute-start(f32[2,136,256]{2,1,0:T(8,128)S(1)} %shard_map.67), channel_id=1, source_target_pairs={{0,1},{1,0},{2,3},{3,2},{4,5},{5,4},{6,7},{7,6},{8,9},{9,8},{10,11... | collective-permute-start | bytes 835592 | tf_op jit(solution)/shard_map/ppermute | solution.py:157
  10.1 0.3 %collective-permute-done.4.theirs = f32[2,136,256]{2,1,0:T(8,128)S(1)} collective-permute-done((f32[2,136,256]{2,1,0:T(8,128)S(1)}, f32[2,136,256]{2,1,0:T(8,128)S(1)}, u32[]{:S(2)}, u32[]{:S(2)}) %collective-permute-start.4) | collective-permute-done | bytes 278560 | tf_op jit(solution)/shard_map/ppermute | solution.py:157
  10.5 2.0 %collective-permute-start.5 = (bf16[136,256]{1,0:T(8,128)(2,1)S(1)}, bf16[136,256]{1,0:T(8,128)(2,1)S(1)}, u32[]{:S(2)}, u32[]{:S(2)}) collective-permute-start(bf16[136,256]{1,0:T(8,128)(2,1)S(1)} %get-tuple-element.20), channel_id=1, source_target_pairs={{0,2},{1,3},{2,6},{3,7},{4,0},{5,1},{6,4},{7,5},{8,10},{9,11},{10,... | collective-permute-start | bytes 208904 | tf_op jit(solution)/shard_map/ppermute | solution.py:154
  12.4 2.5 %collective-permute-start.6 = (bf16[136,256]{1,0:T(8,128)(2,1)S(1)}, bf16[136,256]{1,0:T(8,128)(2,1)S(1)}, u32[]{:S(2)}, u32[]{:S(2)}) collective-permute-start(bf16[136,256]{1,0:T(8,128)(2,1)S(1)} %get-tuple-element.21), channel_id=1, source_target_pairs={{0,6},{1,7},{2,4},{3,5},{4,2},{5,3},{6,0},{7,1},{8,14},{9,15},{10,... | collective-permute-start | bytes 208904 | tf_op jit(solution)/shard_map/ppermute | solution.py:154
  14.9 0.0 collective-permute-done.3.theirs
  14.9 1.6 %collective-permute-start.7 = (bf16[136,256]{1,0:T(8,128)(2,1)S(1)}, bf16[136,256]{1,0:T(8,128)(2,1)S(1)}, u32[]{:S(2)}, u32[]{:S(2)}) collective-permute-start(bf16[136,256]{1,0:T(8,128)(2,1)S(1)} %get-tuple-element.22), channel_id=1, source_target_pairs={{0,4},{1,5},{2,0},{3,1},{4,6},{5,7},{6,2},{7,3},{8,12},{9,13},{10,... | collective-permute-start | bytes 208904 | tf_op jit(solution)/shard_map/ppermute | solution.py:154
  16.6 0.0 collective-permute-done.5.refs_0_
  16.6 2.8 %collective-permute-done.6.refs_1_ = bf16[136,256]{1,0:T(8,128)(2,1)S(1)} collective-permute-done((bf16[136,256]{1,0:T(8,128)(2,1)S(1)}, bf16[136,256]{1,0:T(8,128)(2,1)S(1)}, u32[]{:S(2)}, u32[]{:S(2)}) %collective-permute-start.6) | collective-permute-done | bytes 69664 | tf_op jit(solution)/shard_map/ppermute | solution.py:154
  19.4 0.5 %collective-permute-done.7.last = bf16[136,256]{1,0:T(8,128)(2,1)S(1)} collective-permute-done((bf16[136,256]{1,0:T(8,128)(2,1)S(1)}, bf16[136,256]{1,0:T(8,128)(2,1)S(1)}, u32[]{:S(2)}, u32[]{:S(2)}) %collective-permute-start.7) | collective-permute-done | bytes 69664 | tf_op jit(solution)/shard_map/ppermute | solution.py:154
  19.9 0.9 %shard_map.71 = bf16[128,256]{1,0:T(8,128)(2,1)} custom-call(f32[136,256]{1,0:T(8,128)S(1)} %shard_map.70.earlier, bf16[136,256]{1,0:T(8,128)(2,1)S(1)} %collective-permute-done.7.last, bf16[128,256]{1,0:T(8,128)(2,1)S(1)} %get-tuple-element.18.refs_3_.refs_2_.feats, bf16[256,256]{1,0:T(8,128)(2,1)S(1)} %get-tuple-element.23.weight, ...), custom_call_target="tpu_custom_call" | custom-call | tf_op jit(solution)/shard_map/pallas_call | solution.py:227
  (3 shorter events, 0.1 us)
Async XLA Ops:
  0.0 8.5 %collective-permute-start = (bf16[128,256]{1,0:T(8,128)(2,1)}, bf16[128,256]{1,0:T(8,128)(2,1)S(1)}, u32[]{:S(2)}, u32[]{:S(2)}) collective-permute-start(bf16[128,256]{1,0:T(8,128)(2,1)} %feats_in.1), channel_id=1, source_target_pairs={{0,8},{8,24},{16,0},{24,16},{1,9},{9,25},{17,1},{25,17},{2,10},{10... | collective-permute-start | bytes 196616 | tf_op jit(solution)/shard_map/ppermute | solution.py:150
  2.9 5.5 %collective-permute-start.2 = (bf16[128,256]{1,0:T(8,128)(2,1)}, bf16[128,256]{1,0:T(8,128)(2,1)S(1)}, u32[]{:S(2)}, u32[]{:S(2)}) collective-permute-start(bf16[128,256]{1,0:T(8,128)(2,1)} %feats_in.1), channel_id=1, source_target_pairs={{0,16},{8,0},{16,24},{24,8},{1,17},{9,1},{17,25},{25,9},{2,18},{10... | collective-permute-start | bytes 196616 | tf_op jit(solution)/shard_map/ppermute | solution.py:150
  3.0 5.5 %collective-permute-start.1 = (bf16[128,256]{1,0:T(8,128)(2,1)}, bf16[128,256]{1,0:T(8,128)(2,1)S(1)}, u32[]{:S(2)}, u32[]{:S(2)}) collective-permute-start(bf16[128,256]{1,0:T(8,128)(2,1)} %feats_in.1), channel_id=1, source_target_pairs={{0,24},{8,16},{16,8},{24,0},{1,25},{9,17},{17,9},{25,1},{2,26},{10... | collective-permute-start | bytes 196616 | tf_op jit(solution)/shard_map/ppermute | solution.py:150
  8.8 1.6 %collective-permute-start.4 = (f32[2,136,256]{2,1,0:T(8,128)S(1)}, f32[2,136,256]{2,1,0:T(8,128)S(1)}, u32[]{:S(2)}, u32[]{:S(2)}) collective-permute-start(f32[2,136,256]{2,1,0:T(8,128)S(1)} %shard_map.65.refs_7_), channel_id=1, source_target_pairs={{0,1},{1,0},{2,3},{3,2},{4,5},{5,4},{6,7},{7,6},{8,9},{9,8},{10,11... | collective-permute-start | bytes 835592 | tf_op jit(solution)/shard_map/ppermute | solution.py:157
  9.6 5.3 %collective-permute-start.3 = (f32[2,136,256]{2,1,0:T(8,128)S(1)}, f32[2,136,256]{2,1,0:T(8,128)S(1)}, u32[]{:S(2)}, u32[]{:S(2)}) collective-permute-start(f32[2,136,256]{2,1,0:T(8,128)S(1)} %shard_map.67), channel_id=1, source_target_pairs={{0,1},{1,0},{2,3},{3,2},{4,5},{5,4},{6,7},{7,6},{8,9},{9,8},{10,11... | collective-permute-start | bytes 835592 | tf_op jit(solution)/shard_map/ppermute | solution.py:157
  10.5 6.1 %collective-permute-start.5 = (bf16[136,256]{1,0:T(8,128)(2,1)S(1)}, bf16[136,256]{1,0:T(8,128)(2,1)S(1)}, u32[]{:S(2)}, u32[]{:S(2)}) collective-permute-start(bf16[136,256]{1,0:T(8,128)(2,1)S(1)} %get-tuple-element.20), channel_id=1, source_target_pairs={{0,2},{1,3},{2,6},{3,7},{4,0},{5,1},{6,4},{7,5},{8,10},{9,11},{10,... | collective-permute-start | bytes 208904 | tf_op jit(solution)/shard_map/ppermute | solution.py:154
  12.4 7.0 %collective-permute-start.6 = (bf16[136,256]{1,0:T(8,128)(2,1)S(1)}, bf16[136,256]{1,0:T(8,128)(2,1)S(1)}, u32[]{:S(2)}, u32[]{:S(2)}) collective-permute-start(bf16[136,256]{1,0:T(8,128)(2,1)S(1)} %get-tuple-element.21), channel_id=1, source_target_pairs={{0,6},{1,7},{2,4},{3,5},{4,2},{5,3},{6,0},{7,1},{8,14},{9,15},{10,... | collective-permute-start | bytes 208904 | tf_op jit(solution)/shard_map/ppermute | solution.py:154
  14.9 5.0 %collective-permute-start.7 = (bf16[136,256]{1,0:T(8,128)(2,1)S(1)}, bf16[136,256]{1,0:T(8,128)(2,1)S(1)}, u32[]{:S(2)}, u32[]{:S(2)}) collective-permute-start(bf16[136,256]{1,0:T(8,128)(2,1)S(1)} %get-tuple-element.22), channel_id=1, source_target_pairs={{0,4},{1,5},{2,0},{3,1},{4,6},{5,7},{6,2},{7,3},{8,12},{9,13},{10,... | collective-permute-start | bytes 208904 | tf_op jit(solution)/shard_map/ppermute | solution.py:154

commit v7 on v5

--- a/solution.py
+++ b/solution.py
@@ -91,14 +91,20 @@
         copy.wait()
 
 
-def aggregate_kernel(nodes, chips, slots, mine, steps, *refs):
-    chosen, adjacency, degree = refs[:3]
-    feats_in = refs[3 : 3 + nodes]
-    out, rows = refs[-2:]
+def stack_kernel(steps, nodes, *refs):
+    *feats_in, rows = refs
     node = lax.axis_index("node")
-    tile = feats_in[0].shape[0]
-    for step in range(nodes):
-        rows[along_ring(node, (nodes - step) % nodes, nodes)] = feats_in[step][...]
+    for feats, step in zip(feats_in, steps):
+        rows[along_ring(node, (nodes - step) % nodes, nodes)] = feats[...]
+
+
+def aggregate_kernel(nodes, chips, slots, mine, steps, late, *refs):
+    chosen, adjacency, degree, rows = refs[:4]
+    out = refs[-1]
+    if late is not None:
+        out, rows = refs[-2:]
+        rows[along_ring(lax.axis_index("node"), (nodes - late) % nodes, nodes)] = refs[4][...]
+    tile = rows.shape[1]
     for index, step in enumerate(steps):
         place = mine * chips + step
         picks = [chosen[place * slots + slot, 0] for slot in range(slots)]
@@ -186,17 +192,30 @@
     )
     rows_in = [own_feats] + rows_in
 
-    def aggregate(mine, steps, *after):
+    late = nodes // 2
+    early = [step for step in range(nodes) if step != late]
+    stack = jax.ShapeDtypeStruct((nodes, tile, width), jnp.bfloat16)
+    rows = pl.pallas_call(
+        functools.partial(stack_kernel, early, nodes),
+        out_shape=stack,
+        in_specs=[VMEM] * len(early),
+        out_specs=VMEM,
+        compiler_params=PARAMS,
+    )(*(rows_in[step] for step in early))
+
+    def aggregate(mine, steps, rows, *more, late=None):
         dtype = jnp.float32 if mine else jnp.bfloat16
+        out = jax.ShapeDtypeStruct((len(steps), tile + EXTRA, width), dtype)
+        first = late is not None
         return pl.pallas_call(
-            functools.partial(aggregate_kernel, nodes, chips, slots, mine, steps),
-            out_shape=jax.ShapeDtypeStruct((len(steps), tile + EXTRA, width), dtype),
-            in_specs=[VMEM] * (3 + nodes + len(after)),
-            out_specs=VMEM,
-            scratch_shapes=[pltpu.VMEM((nodes, tile, width), jnp.bfloat16)],
+            functools.partial(aggregate_kernel, nodes, chips, slots, mine, steps, late),
+            out_shape=[out, stack] if first else out,
+            in_specs=[VMEM] * (4 + len(more)),
+            out_specs=[VMEM] * 2 if first else VMEM,
+            input_output_aliases={3: 1} if first else {},
             compiler_params=PARAMS,
             cost_estimate=pl.CostEstimate(flops=1 << 27, bytes_accessed=1 << 22, transcendentals=0),
-        )(chosen, adjacency, degree, *rows_in, *after)
+        )(chosen, adjacency, degree, rows, *more)
 
     def merge(first, mine, theirs, dtypes, *after):
         return pl.pallas_call(
@@ -209,9 +228,9 @@
 
     cut = min(chips, FIRST + 1)
     far, near = list(range(1, cut)), list(range(cut, chips)) + [0]
-    first = aggregate(0, far)
-    mine = aggregate(1, far + near, first)
-    second = aggregate(0, near, mine)
+    first, rows = aggregate(0, far, rows, rows_in[late], late=late)
+    mine = aggregate(1, far + near, rows, first)
+    second = aggregate(0, near, rows, mine)
     parts = merge(0, mine, over_cores(first), [jnp.bfloat16] * len(far))
     *rest, own = merge(
         len(far), mine, over_cores(second), [jnp.bfloat16] * (len(near) - 1) + [jnp.float32]

time: 20.8 us -> 20.7 us (level)
  no operation moved by 1% of the time
where the time goes in v7:
time: 20.7 us; the launch traced here: 20.6 us
  starting transfers between devices  12.6 us (61%)
  Pallas kernels  4.47 us (22%)
  waiting for transfers between devices  3.47 us (17%)
    ppermute x3, starting transfers between devices, over_chips(): return lax.ppermute(array, 'feat', pairs)  6.01 us
    ppermute x3, starting transfers between devices, over_nodes(): return lax.ppermute(feats, 'node', pairs)  5.92 us
    ppermute x3, waiting for transfers between devices, over_chips(): return lax.ppermute(array, 'feat', pairs)  3.3 us
    pallas_call x1, Pallas kernels, body(): pl.pallas_call(prepare_kernel, out_shape=[jax.ShapeDtypeStruct((groups, t...  2.54 us
    pallas_call x3, Pallas kernels, aggregate(): pl.pallas_call(functools.partial(aggregate_kernel, nodes, chips, slots, m...  0.89 us
    pallas_call x1, Pallas kernels, body(): pl.pallas_call(update_kernel, out_shape=jax.ShapeDtypeStruct((tile, width...  0.87 us
    ppermute x2, starting transfers between devices, over_cores(): return lax.ppermute(array, 'feat', [(f, f ^ 1) for f in range(2 * chips)])  0.63 us
  transfers between devices with their start and end apart: 8, of which 3 were waited for; matrix products, arithmetic and copies ran while one was open for 0% of the time, Pallas kernels for 16%

profile of v7, /device:TPU:0, one launch (start us, length us, event | category | flops | bytes accessed | tf_op | source)
XLA Modules:
  0.0 20.6 jit_solution(15914773481416873977)
XLA Ops:
  0.0 2.9 %collective-permute-start = (bf16[128,256]{1,0:T(8,128)(2,1)}, bf16[128,256]{1,0:T(8,128)(2,1)S(1)}, u32[]{:S(2)}, u32[]{:S(2)}) collective-permute-start(bf16[128,256]{1,0:T(8,128)(2,1)} %feats_in.1), channel_id=1, source_target_pairs={{0,8},{8,24},{16,0},{24,16},{1,9},{9,25},{17,1},{25,17},{2,10},{10... | collective-permute-start | bytes 196616 | tf_op jit(solution)/shard_map/ppermute | solution.py:156
  2.9 0.0 collective-permute-start.1
  3.0 3.0 %collective-permute-start.2 = (bf16[128,256]{1,0:T(8,128)(2,1)}, bf16[128,256]{1,0:T(8,128)(2,1)S(1)}, u32[]{:S(2)}, u32[]{:S(2)}) collective-permute-start(bf16[128,256]{1,0:T(8,128)(2,1)} %feats_in.1), channel_id=1, source_target_pairs={{0,24},{8,16},{16,8},{24,0},{1,25},{9,17},{17,9},{25,1},{2,26},{10... | collective-permute-start | bytes 196616 | tf_op jit(solution)/shard_map/ppermute | solution.py:156
  5.9 2.5 %shard_map.64 = (bf16[8,128,384]{2,1,0:T(8,128)(2,1)S(1)}, f32[8,8,128]{2,1,0:T(8,128)S(1)}, s32[24,128]{1,0:T(8,128)S(1)}, bf16[128,256]{1,0:T(8,128)(2,1)S(1)}...) custom-call(s32[1,8]{1,0:T(1,128)} %bitcast.5, s32[3,8]{1,0:T(4,128)} %bitcast.3, bf16[8,3,128,128]{3,2,1,0:T(8,128)(2,1)} %tiles_in.1, ...), custom_call_target="tpu_custom_call" | custom-call | flops 134217728 | bytes 4194304 | tf_op jit(solution)/shard_map/pallas_call | solution.py:166
  8.5 0.0 collective-permute-done.refs_1_
  8.5 0.0 collective-permute-done.1.refs_2_
  8.5 0.1 shard_map.65.refs_3_
  8.6 0.0 collective-permute-done.2.refs_4_
  8.6 0.3 %shard_map.66 = (bf16[2,136,256]{2,1,0:T(8,128)(2,1)S(1)}, bf16[4,128,256]{2,1,0:T(8,128)(2,1)S(1)}) custom-call(s32[24,128]{1,0:T(8,128)S(1)} %get-tuple-element.17.refs_0_, bf16[8,128,384]{2,1,0:T(8,128)(2,1)S(1)} %get-tuple-element.18.refs_1_, f32[8,8,128]{2,1,0:T(8,128)S(1)} %get-tuple-element.19.refs_2_, ...), custom_call_target="tpu_custom_call", output_to_operand_aliasing={{1}: (3, {})} | custom-call | flops 134217728 | bytes 4194304 | tf_op jit(solution)/shard_map/pallas_call | solution.py:210
  8.9 0.1 collective-permute-start.4
  8.9 0.3 %shard_map.67.refs_4_.mine = f32[4,136,256]{2,1,0:T(8,128)S(1)} custom-call(s32[24,128]{1,0:T(8,128)S(1)} %get-tuple-element.17.refs_0_, bf16[8,128,384]{2,1,0:T(8,128)(2,1)S(1)} %get-tuple-element.18.refs_1_, f32[8,8,128]{2,1,0:T(8,128)S(1)} %get-tuple-element.19.refs_2_, bf16[4,128,256]{2,1,0:T(8,128)(2,1)S(1)} %get-tuple-element.21.refs_3_, ...), custom_call_target="tpu_custom_call" | custom-call | flops 134217728 | bytes 4194304 | tf_op jit(solution)/shard_map/pallas_call | solution.py:210
  9.3 0.3 %shard_map.68 = bf16[2,136,256]{2,1,0:T(8,128)(2,1)S(1)} custom-call(s32[24,128]{1,0:T(8,128)S(1)} %get-tuple-element.17.refs_0_, bf16[8,128,384]{2,1,0:T(8,128)(2,1)S(1)} %get-tuple-element.18.refs_1_, f32[8,8,128]{2,1,0:T(8,128)S(1)} %get-tuple-element.19.refs_2_, bf16[4,128,256]{2,1,0:T(8,128)(2,1)S(1)} %get-tuple-element.21.refs_3_, ...), custom_call_target="tpu_custom_call" | custom-call | flops 134217728 | bytes 4194304 | tf_op jit(solution)/shard_map/pallas_call | solution.py:210
  9.6 0.6 %collective-permute-start.3 = (bf16[2,136,256]{2,1,0:T(8,128)(2,1)S(1)}, bf16[2,136,256]{2,1,0:T(8,128)(2,1)S(1)}, u32[]{:S(2)}, u32[]{:S(2)}) collective-permute-start(bf16[2,136,256]{2,1,0:T(8,128)(2,1)S(1)} %shard_map.68), channel_id=1, source_target_pairs={{0,1},{1,0},{2,3},{3,2},{4,5},{5,4},{6,7},{7,6},{8,9},{9,8},{10,11... | collective-permute-start | bytes 417800 | tf_op jit(solution)/shard_map/ppermute | solution.py:163
  10.1 0.2 collective-permute-done.4.theirs
  10.3 1.9 %collective-permute-start.5 = (bf16[136,256]{1,0:T(8,128)(2,1)S(1)}, bf16[136,256]{1,0:T(8,128)(2,1)S(1)}, u32[]{:S(2)}, u32[]{:S(2)}) collective-permute-start(bf16[136,256]{1,0:T(8,128)(2,1)S(1)} %get-tuple-element.24), channel_id=1, source_target_pairs={{0,2},{1,3},{2,6},{3,7},{4,0},{5,1},{6,4},{7,5},{8,10},{9,11},{10,... | collective-permute-start | bytes 208904 | tf_op jit(solution)/shard_map/ppermute | solution.py:160
  12.2 2.5 %collective-permute-start.6 = (bf16[136,256]{1,0:T(8,128)(2,1)S(1)}, bf16[136,256]{1,0:T(8,128)(2,1)S(1)}, u32[]{:S(2)}, u32[]{:S(2)}) collective-permute-start(bf16[136,256]{1,0:T(8,128)(2,1)S(1)} %get-tuple-element.25), channel_id=1, source_target_pairs={{0,6},{1,7},{2,4},{3,5},{4,2},{5,3},{6,0},{7,1},{8,14},{9,15},{10,... | collective-permute-start | bytes 208904 | tf_op jit(solution)/shard_map/ppermute | solution.py:160
  14.7 0.0 collective-permute-done.3.theirs
  14.7 1.6 %collective-permute-start.7 = (bf16[136,256]{1,0:T(8,128)(2,1)S(1)}, bf16[136,256]{1,0:T(8,128)(2,1)S(1)}, u32[]{:S(2)}, u32[]{:S(2)}) collective-permute-start(bf16[136,256]{1,0:T(8,128)(2,1)S(1)} %get-tuple-element.26), channel_id=1, source_target_pairs={{0,4},{1,5},{2,0},{3,1},{4,6},{5,7},{6,2},{7,3},{8,12},{9,13},{10,... | collective-permute-start | bytes 208904 | tf_op jit(solution)/shard_map/ppermute | solution.py:160
  16.4 0.0 collective-permute-done.5.refs_0_
  16.4 2.8 %collective-permute-done.6.refs_1_ = bf16[136,256]{1,0:T(8,128)(2,1)S(1)} collective-permute-done((bf16[136,256]{1,0:T(8,128)(2,1)S(1)}, bf16[136,256]{1,0:T(8,128)(2,1)S(1)}, u32[]{:S(2)}, u32[]{:S(2)}) %collective-permute-start.6) | collective-permute-done | bytes 69664 | tf_op jit(solution)/shard_map/ppermute | solution.py:160
  19.2 0.5 %collective-permute-done.7.last = bf16[136,256]{1,0:T(8,128)(2,1)S(1)} collective-permute-done((bf16[136,256]{1,0:T(8,128)(2,1)S(1)}, bf16[136,256]{1,0:T(8,128)(2,1)S(1)}, u32[]{:S(2)}, u32[]{:S(2)}) %collective-permute-start.7) | collective-permute-done | bytes 69664 | tf_op jit(solution)/shard_map/ppermute | solution.py:160
  19.7 0.9 %shard_map.72 = bf16[128,256]{1,0:T(8,128)(2,1)} custom-call(f32[136,256]{1,0:T(8,128)S(1)} %shard_map.71.earlier, bf16[136,256]{1,0:T(8,128)(2,1)S(1)} %collective-permute-done.7.last, bf16[128,256]{1,0:T(8,128)(2,1)S(1)} %get-tuple-element.20.refs_0_.refs_2_.feats, bf16[256,256]{1,0:T(8,128)(2,1)S(1)} %get-tuple-element.27.weight, ...), custom_call_target="tpu_custom_call" | custom-call | tf_op jit(solution)/shard_map/pallas_call | solution.py:247
  (3 shorter events, 0.1 us)
Async XLA Ops:
  0.0 8.5 %collective-permute-start = (bf16[128,256]{1,0:T(8,128)(2,1)}, bf16[128,256]{1,0:T(8,128)(2,1)S(1)}, u32[]{:S(2)}, u32[]{:S(2)}) collective-permute-start(bf16[128,256]{1,0:T(8,128)(2,1)} %feats_in.1), channel_id=1, source_target_pairs={{0,8},{8,24},{16,0},{24,16},{1,9},{9,25},{17,1},{25,17},{2,10},{10... | collective-permute-start | bytes 196616 | tf_op jit(solution)/shard_map/ppermute | solution.py:156
  2.9 5.5 %collective-permute-start.1 = (bf16[128,256]{1,0:T(8,128)(2,1)}, bf16[128,256]{1,0:T(8,128)(2,1)S(1)}, u32[]{:S(2)}, u32[]{:S(2)}) collective-permute-start(bf16[128,256]{1,0:T(8,128)(2,1)} %feats_in.1), channel_id=1, source_target_pairs={{0,16},{8,0},{16,24},{24,8},{1,17},{9,1},{17,25},{25,9},{2,18},{10... | collective-permute-start | bytes 196616 | tf_op jit(solution)/shard_map/ppermute | solution.py:156
  3.0 5.6 %collective-permute-start.2 = (bf16[128,256]{1,0:T(8,128)(2,1)}, bf16[128,256]{1,0:T(8,128)(2,1)S(1)}, u32[]{:S(2)}, u32[]{:S(2)}) collective-permute-start(bf16[128,256]{1,0:T(8,128)(2,1)} %feats_in.1), channel_id=1, source_target_pairs={{0,24},{8,16},{16,8},{24,0},{1,25},{9,17},{17,9},{25,1},{2,26},{10... | collective-permute-start | bytes 196616 | tf_op jit(solution)/shard_map/ppermute | solution.py:156
  8.9 1.4 %collective-permute-start.4 = (bf16[2,136,256]{2,1,0:T(8,128)(2,1)S(1)}, bf16[2,136,256]{2,1,0:T(8,128)(2,1)S(1)}, u32[]{:S(2)}, u32[]{:S(2)}) collective-permute-start(bf16[2,136,256]{2,1,0:T(8,128)(2,1)S(1)} %get-tuple-element.22.refs_4_), channel_id=1, source_target_pairs={{0,1},{1,0},{2,3},{3,2},{4,5},{5,4},{6,7},{7,6},{8,9},{9,8},{10,11... | collective-permute-start | bytes 417800 | tf_op jit(solution)/shard_map/ppermute | solution.py:163
  9.6 5.1 %collective-permute-start.3 = (bf16[2,136,256]{2,1,0:T(8,128)(2,1)S(1)}, bf16[2,136,256]{2,1,0:T(8,128)(2,1)S(1)}, u32[]{:S(2)}, u32[]{:S(2)}) collective-permute-start(bf16[2,136,256]{2,1,0:T(8,128)(2,1)S(1)} %shard_map.68), channel_id=1, source_target_pairs={{0,1},{1,0},{2,3},{3,2},{4,5},{5,4},{6,7},{7,6},{8,9},{9,8},{10,11... | collective-permute-start | bytes 417800 | tf_op jit(solution)/shard_map/ppermute | solution.py:163
  10.3 6.1 %collective-permute-start.5 = (bf16[136,256]{1,0:T(8,128)(2,1)S(1)}, bf16[136,256]{1,0:T(8,128)(2,1)S(1)}, u32[]{:S(2)}, u32[]{:S(2)}) collective-permute-start(bf16[136,256]{1,0:T(8,128)(2,1)S(1)} %get-tuple-element.24), channel_id=1, source_target_pairs={{0,2},{1,3},{2,6},{3,7},{4,0},{5,1},{6,4},{7,5},{8,10},{9,11},{10,... | collective-permute-start | bytes 208904 | tf_op jit(solution)/shard_map/ppermute | solution.py:160
  12.2 7.0 %collective-permute-start.6 = (bf16[136,256]{1,0:T(8,128)(2,1)S(1)}, bf16[136,256]{1,0:T(8,128)(2,1)S(1)}, u32[]{:S(2)}, u32[]{:S(2)}) collective-permute-start(bf16[136,256]{1,0:T(8,128)(2,1)S(1)} %get-tuple-element.25), channel_id=1, source_target_pairs={{0,6},{1,7},{2,4},{3,5},{4,2},{5,3},{6,0},{7,1},{8,14},{9,15},{10,... | collective-permute-start | bytes 208904 | tf_op jit(solution)/shard_map/ppermute | solution.py:160
  14.7 5.0 %collective-permute-start.7 = (bf16[136,256]{1,0:T(8,128)(2,1)S(1)}, bf16[136,256]{1,0:T(8,128)(2,1)S(1)}, u32[]{:S(2)}, u32[]{:S(2)}) collective-permute-start(bf16[136,256]{1,0:T(8,128)(2,1)S(1)} %get-tuple-element.26), channel_id=1, source_target_pairs={{0,4},{1,5},{2,0},{3,1},{4,6},{5,7},{6,2},{7,3},{8,12},{9,13},{10,... | collective-permute-start | bytes 208904 | tf_op jit(solution)/shard_map/ppermute | solution.py:160

commit v8 on v7

--- a/solution.py
+++ b/solution.py
@@ -192,7 +192,7 @@
     )
     rows_in = [own_feats] + rows_in
 
-    late = nodes // 2
+    late = 1
     early = [step for step in range(nodes) if step != late]
     stack = jax.ShapeDtypeStruct((nodes, tile, width), jnp.bfloat16)
     rows = pl.pallas_call(

time: 20.7 us -> 20.8 us (level)
  waiting for transfers between devices: 3.47 us -> 3.78 us
  starting transfers between devices: 12.6 us -> 12.3 us
    ppermute x3, waiting for transfers between devices: 0.01 us -> 0.32 us  [over_nodes(): return lax.ppermute(feats, 'node', pairs)]
    ppermute x3, starting transfers between devices: 6.01 us -> 5.73 us  [over_chips(): return lax.ppermute(array, 'feat', pairs)]
  transfers between devices with their start and end apart: 8 -> 8, of which waited for: 3 -> 4; matrix products, arithmetic and copies ran while one was open for 0% -> 0% of each run, Pallas kernels for 16% -> 16%
where the time goes in v8:
time: 20.8 us; the launch traced here: 20.6 us
  starting transfers between devices  12.3 us (59%)
  Pallas kernels  4.46 us (21%)
  waiting for transfers between devices  3.78 us (18%)
    ppermute x3, starting transfers between devices, over_nodes(): return lax.ppermute(feats, 'node', pairs)  5.92 us
    ppermute x3, starting transfers between devices, over_chips(): return lax.ppermute(array, 'feat', pairs)  5.73 us
    ppermute x3, waiting for transfers between devices, over_chips(): return lax.ppermute(array, 'feat', pairs)  3.3 us
    pallas_call x1, Pallas kernels, body(): pl.pallas_call(prepare_kernel, out_shape=[jax.ShapeDtypeStruct((groups, t...  2.54 us
    pallas_call x3, Pallas kernels, aggregate(): pl.pallas_call(functools.partial(aggregate_kernel, nodes, chips, slots, m...  0.88 us
    pallas_call x1, Pallas kernels, body(): pl.pallas_call(update_kernel, out_shape=jax.ShapeDtypeStruct((tile, width...  0.87 us
    ppermute x2, starting transfers between devices, over_cores(): return lax.ppermute(array, 'feat', [(f, f ^ 1) for f in range(2 * chips)])  0.63 us
  transfers between devices with their start and end apart: 8, of which 4 were waited for; matrix products, arithmetic and copies ran while one was open for 0% of the time, Pallas kernels for 16%

profile of v8, /device:TPU:0, one launch (start us, length us, event | category | flops | bytes accessed | tf_op | source)
XLA Modules:
  0.0 20.6 jit_solution(4507227171493867852)
XLA Ops:
  0.0 3.9 %collective-permute-start = (bf16[128,256]{1,0:T(8,128)(2,1)}, bf16[128,256]{1,0:T(8,128)(2,1)S(1)}, u32[]{:S(2)}, u32[]{:S(2)}) collective-permute-start(bf16[128,256]{1,0:T(8,128)(2,1)} %feats_in.1), channel_id=1, source_target_pairs={{0,24},{8,16},{16,8},{24,0},{1,25},{9,17},{17,9},{25,1},{2,26},{10... | collective-permute-start | bytes 196616 | tf_op jit(solution)/shard_map/ppermute | solution.py:156
  3.9 0.5 %collective-permute-start.1 = (bf16[128,256]{1,0:T(8,128)(2,1)}, bf16[128,256]{1,0:T(8,128)(2,1)S(1)}, u32[]{:S(2)}, u32[]{:S(2)}) collective-permute-start(bf16[128,256]{1,0:T(8,128)(2,1)} %feats_in.1), channel_id=1, source_target_pairs={{0,16},{8,0},{16,24},{24,8},{1,17},{9,1},{17,25},{25,9},{2,18},{10... | collective-permute-start | bytes 196616 | tf_op jit(solution)/shard_map/ppermute | solution.py:156
  4.4 1.5 %collective-permute-start.2 = (bf16[128,256]{1,0:T(8,128)(2,1)}, bf16[128,256]{1,0:T(8,128)(2,1)S(1)}, u32[]{:S(2)}, u32[]{:S(2)}) collective-permute-start(bf16[128,256]{1,0:T(8,128)(2,1)} %feats_in.1), channel_id=1, source_target_pairs={{0,8},{8,24},{16,0},{24,16},{1,9},{9,25},{17,1},{25,17},{2,10},{10... | collective-permute-start | bytes 196616 | tf_op jit(solution)/shard_map/ppermute | solution.py:156
  5.9 2.5 %shard_map.64 = (bf16[8,128,384]{2,1,0:T(8,128)(2,1)S(1)}, f32[8,8,128]{2,1,0:T(8,128)S(1)}, s32[24,128]{1,0:T(8,128)S(1)}, bf16[128,256]{1,0:T(8,128)(2,1)S(1)}...) custom-call(s32[1,8]{1,0:T(1,128)} %bitcast.5, s32[3,8]{1,0:T(4,128)} %bitcast.3, bf16[8,3,128,128]{3,2,1,0:T(8,128)(2,1)} %tiles_in.1, ...), custom_call_target="tpu_custom_call" | custom-call | flops 134217728 | bytes 4194304 | tf_op jit(solution)/shard_map/pallas_call | solution.py:166
  8.5 0.0 collective-permute-done.refs_1_
  8.5 0.0 collective-permute-done.1.refs_2_
  8.5 0.1 shard_map.65.refs_3_
  8.6 0.3 %collective-permute-done.2.refs_4_ = bf16[128,256]{1,0:T(8,128)(2,1)S(1)} collective-permute-done((bf16[128,256]{1,0:T(8,128)(2,1)}, bf16[128,256]{1,0:T(8,128)(2,1)S(1)}, u32[]{:S(2)}, u32[]{:S(2)}) %collective-permute-start.2) | collective-permute-done | bytes 65568 | tf_op jit(solution)/shard_map/ppermute | solution.py:156
  8.9 0.3 %shard_map.66 = (bf16[2,136,256]{2,1,0:T(8,128)(2,1)S(1)}, bf16[4,128,256]{2,1,0:T(8,128)(2,1)S(1)}) custom-call(s32[24,128]{1,0:T(8,128)S(1)} %get-tuple-element.17.refs_0_, bf16[8,128,384]{2,1,0:T(8,128)(2,1)S(1)} %get-tuple-element.18.refs_1_, f32[8,8,128]{2,1,0:T(8,128)S(1)} %get-tuple-element.19.refs_2_, ...), custom_call_target="tpu_custom_call", output_to_operand_aliasing={{1}: (3, {})} | custom-call | flops 134217728 | bytes 4194304 | tf_op jit(solution)/shard_map/pallas_call | solution.py:210
  9.2 0.1 collective-permute-start.4
  9.2 0.3 %shard_map.67.refs_4_.mine = f32[4,136,256]{2,1,0:T(8,128)S(1)} custom-call(s32[24,128]{1,0:T(8,128)S(1)} %get-tuple-element.17.refs_0_, bf16[8,128,384]{2,1,0:T(8,128)(2,1)S(1)} %get-tuple-element.18.refs_1_, f32[8,8,128]{2,1,0:T(8,128)S(1)} %get-tuple-element.19.refs_2_, bf16[4,128,256]{2,1,0:T(8,128)(2,1)S(1)} %get-tuple-element.21.refs_3_, ...), custom_call_target="tpu_custom_call" | custom-call | flops 134217728 | bytes 4194304 | tf_op jit(solution)/shard_map/pallas_call | solution.py:210
  9.6 0.3 %shard_map.68 = bf16[2,136,256]{2,1,0:T(8,128)(2,1)S(1)} custom-call(s32[24,128]{1,0:T(8,128)S(1)} %get-tuple-element.17.refs_0_, bf16[8,128,384]{2,1,0:T(8,128)(2,1)S(1)} %get-tuple-element.18.refs_1_, f32[8,8,128]{2,1,0:T(8,128)S(1)} %get-tuple-element.19.refs_2_, bf16[4,128,256]{2,1,0:T(8,128)(2,1)S(1)} %get-tuple-element.21.refs_3_, ...), custom_call_target="tpu_custom_call" | custom-call | flops 134217728 | bytes 4194304 | tf_op jit(solution)/shard_map/pallas_call | solution.py:210
  9.9 0.6 %collective-permute-start.3 = (bf16[2,136,256]{2,1,0:T(8,128)(2,1)S(1)}, bf16[2,136,256]{2,1,0:T(8,128)(2,1)S(1)}, u32[]{:S(2)}, u32[]{:S(2)}) collective-permute-start(bf16[2,136,256]{2,1,0:T(8,128)(2,1)S(1)} %shard_map.68), channel_id=1, source_target_pairs={{0,1},{1,0},{2,3},{3,2},{4,5},{5,4},{6,7},{7,6},{8,9},{9,8},{10,11... | collective-permute-start | bytes 417800 | tf_op jit(solution)/shard_map/ppermute | solution.py:163
  10.4 0.2 collective-permute-done.4.theirs
  10.6 1.6 %collective-permute-start.5 = (bf16[136,256]{1,0:T(8,128)(2,1)S(1)}, bf16[136,256]{1,0:T(8,128)(2,1)S(1)}, u32[]{:S(2)}, u32[]{:S(2)}) collective-permute-start(bf16[136,256]{1,0:T(8,128)(2,1)S(1)} %get-tuple-element.24), channel_id=1, source_target_pairs={{0,2},{1,3},{2,6},{3,7},{4,0},{5,1},{6,4},{7,5},{8,10},{9,11},{10,... | collective-permute-start | bytes 208904 | tf_op jit(solution)/shard_map/ppermute | solution.py:160
  12.3 2.5 %collective-permute-start.6 = (bf16[136,256]{1,0:T(8,128)(2,1)S(1)}, bf16[136,256]{1,0:T(8,128)(2,1)S(1)}, u32[]{:S(2)}, u32[]{:S(2)}) collective-permute-start(bf16[136,256]{1,0:T(8,128)(2,1)S(1)} %get-tuple-element.25), channel_id=1, source_target_pairs={{0,6},{1,7},{2,4},{3,5},{4,2},{5,3},{6,0},{7,1},{8,14},{9,15},{10,... | collective-permute-start | bytes 208904 | tf_op jit(solution)/shard_map/ppermute | solution.py:160
  14.7 0.0 collective-permute-done.3.theirs
  14.8 1.6 %collective-permute-start.7 = (bf16[136,256]{1,0:T(8,128)(2,1)S(1)}, bf16[136,256]{1,0:T(8,128)(2,1)S(1)}, u32[]{:S(2)}, u32[]{:S(2)}) collective-permute-start(bf16[136,256]{1,0:T(8,128)(2,1)S(1)} %get-tuple-element.26), channel_id=1, source_target_pairs={{0,4},{1,5},{2,0},{3,1},{4,6},{5,7},{6,2},{7,3},{8,12},{9,13},{10,... | collective-permute-start | bytes 208904 | tf_op jit(solution)/shard_map/ppermute | solution.py:160
  16.4 0.0 collective-permute-done.5.refs_0_
  16.4 2.8 %collective-permute-done.6.refs_1_ = bf16[136,256]{1,0:T(8,128)(2,1)S(1)} collective-permute-done((bf16[136,256]{1,0:T(8,128)(2,1)S(1)}, bf16[136,256]{1,0:T(8,128)(2,1)S(1)}, u32[]{:S(2)}, u32[]{:S(2)}) %collective-permute-start.6) | collective-permute-done | bytes 69664 | tf_op jit(solution)/shard_map/ppermute | solution.py:160
  19.3 0.5 %collective-permute-done.7.last = bf16[136,256]{1,0:T(8,128)(2,1)S(1)} collective-permute-done((bf16[136,256]{1,0:T(8,128)(2,1)S(1)}, bf16[136,256]{1,0:T(8,128)(2,1)S(1)}, u32[]{:S(2)}, u32[]{:S(2)}) %collective-permute-start.7) | collective-permute-done | bytes 69664 | tf_op jit(solution)/shard_map/ppermute | solution.py:160
  19.7 0.9 %shard_map.72 = bf16[128,256]{1,0:T(8,128)(2,1)} custom-call(f32[136,256]{1,0:T(8,128)S(1)} %shard_map.71.earlier, bf16[136,256]{1,0:T(8,128)(2,1)S(1)} %collective-permute-done.7.last, bf16[128,256]{1,0:T(8,128)(2,1)S(1)} %get-tuple-element.20.refs_0_.refs_2_.feats, bf16[256,256]{1,0:T(8,128)(2,1)S(1)} %get-tuple-element.27.weight, ...), custom_call_target="tpu_custom_call" | custom-call | tf_op jit(solution)/shard_map/pallas_call | solution.py:247
  (3 shorter events, 0.1 us)
Async XLA Ops:
  0.0 8.5 %collective-permute-start = (bf16[128,256]{1,0:T(8,128)(2,1)}, bf16[128,256]{1,0:T(8,128)(2,1)S(1)}, u32[]{:S(2)}, u32[]{:S(2)}) collective-permute-start(bf16[128,256]{1,0:T(8,128)(2,1)} %feats_in.1), channel_id=1, source_target_pairs={{0,24},{8,16},{16,8},{24,0},{1,25},{9,17},{17,9},{25,1},{2,26},{10... | collective-permute-start | bytes 196616 | tf_op jit(solution)/shard_map/ppermute | solution.py:156
  3.9 4.6 %collective-permute-start.1 = (bf16[128,256]{1,0:T(8,128)(2,1)}, bf16[128,256]{1,0:T(8,128)(2,1)S(1)}, u32[]{:S(2)}, u32[]{:S(2)}) collective-permute-start(bf16[128,256]{1,0:T(8,128)(2,1)} %feats_in.1), channel_id=1, source_target_pairs={{0,16},{8,0},{16,24},{24,8},{1,17},{9,1},{17,25},{25,9},{2,18},{10... | collective-permute-start | bytes 196616 | tf_op jit(solution)/shard_map/ppermute | solution.py:156
  4.4 4.5 %collective-permute-start.2 = (bf16[128,256]{1,0:T(8,128)(2,1)}, bf16[128,256]{1,0:T(8,128)(2,1)S(1)}, u32[]{:S(2)}, u32[]{:S(2)}) collective-permute-start(bf16[128,256]{1,0:T(8,128)(2,1)} %feats_in.1), channel_id=1, source_target_pairs={{0,8},{8,24},{16,0},{24,16},{1,9},{9,25},{17,1},{25,17},{2,10},{10... | collective-permute-start | bytes 196616 | tf_op jit(solution)/shard_map/ppermute | solution.py:156
  9.2 1.4 %collective-permute-start.4 = (bf16[2,136,256]{2,1,0:T(8,128)(2,1)S(1)}, bf16[2,136,256]{2,1,0:T(8,128)(2,1)S(1)}, u32[]{:S(2)}, u32[]{:S(2)}) collective-permute-start(bf16[2,136,256]{2,1,0:T(8,128)(2,1)S(1)} %get-tuple-element.22.refs_4_), channel_id=1, source_target_pairs={{0,1},{1,0},{2,3},{3,2},{4,5},{5,4},{6,7},{7,6},{8,9},{9,8},{10,11... | collective-permute-start | bytes 417800 | tf_op jit(solution)/shard_map/ppermute | solution.py:163
  9.9 4.9 %collective-permute-start.3 = (bf16[2,136,256]{2,1,0:T(8,128)(2,1)S(1)}, bf16[2,136,256]{2,1,0:T(8,128)(2,1)S(1)}, u32[]{:S(2)}, u32[]{:S(2)}) collective-permute-start(bf16[2,136,256]{2,1,0:T(8,128)(2,1)S(1)} %shard_map.68), channel_id=1, source_target_pairs={{0,1},{1,0},{2,3},{3,2},{4,5},{5,4},{6,7},{7,6},{8,9},{9,8},{10,11... | collective-permute-start | bytes 417800 | tf_op jit(solution)/shard_map/ppermute | solution.py:163
  10.6 5.8 %collective-permute-start.5 = (bf16[136,256]{1,0:T(8,128)(2,1)S(1)}, bf16[136,256]{1,0:T(8,128)(2,1)S(1)}, u32[]{:S(2)}, u32[]{:S(2)}) collective-permute-start(bf16[136,256]{1,0:T(8,128)(2,1)S(1)} %get-tuple-element.24), channel_id=1, source_target_pairs={{0,2},{1,3},{2,6},{3,7},{4,0},{5,1},{6,4},{7,5},{8,10},{9,11},{10,... | collective-permute-start | bytes 208904 | tf_op jit(solution)/shard_map/ppermute | solution.py:160
  12.3 7.0 %collective-permute-start.6 = (bf16[136,256]{1,0:T(8,128)(2,1)S(1)}, bf16[136,256]{1,0:T(8,128)(2,1)S(1)}, u32[]{:S(2)}, u32[]{:S(2)}) collective-permute-start(bf16[136,256]{1,0:T(8,128)(2,1)S(1)} %get-tuple-element.25), channel_id=1, source_target_pairs={{0,6},{1,7},{2,4},{3,5},{4,2},{5,3},{6,0},{7,1},{8,14},{9,15},{10,... | collective-permute-start | bytes 208904 | tf_op jit(solution)/shard_map/ppermute | solution.py:160
  14.8 5.0 %collective-permute-start.7 = (bf16[136,256]{1,0:T(8,128)(2,1)S(1)}, bf16[136,256]{1,0:T(8,128)(2,1)S(1)}, u32[]{:S(2)}, u32[]{:S(2)}) collective-permute-start(bf16[136,256]{1,0:T(8,128)(2,1)S(1)} %get-tuple-element.26), channel_id=1, source_target_pairs={{0,4},{1,5},{2,0},{3,1},{4,6},{5,7},{6,2},{7,3},{8,12},{9,13},{10,... | collective-permute-start | bytes 208904 | tf_op jit(solution)/shard_map/ppermute | solution.py:160

commit v9 on v5

--- a/solution.py
+++ b/solution.py
@@ -108,12 +108,12 @@
         out[index, tile:] = split_rows(degree[place]).astype(out.dtype)
 
 
-def merge_kernel(first, count, mine, theirs, *outs):
+def merge_kernel(first, skip, count, mine, theirs, *outs):
     outs = outs[-count:]
     tile = mine.shape[1] - EXTRA
     for index, out in enumerate(outs):
-        total = mine[first + index, :tile] + theirs[index, :tile].astype(jnp.float32)
-        degree = split_rows(join_rows(mine[first + index, tile:]) + join_rows(theirs[index, tile:]))
+        total = mine[first + index, :tile] + theirs[skip + index, :tile].astype(jnp.float32)
+        degree = split_rows(join_rows(mine[first + index, tile:]) + join_rows(theirs[skip + index, tile:]))
         out[:tile] = total.astype(out.dtype)
         out[tile:] = degree.astype(out.dtype)
 
@@ -198,9 +198,9 @@
             cost_estimate=pl.CostEstimate(flops=1 << 27, bytes_accessed=1 << 22, transcendentals=0),
         )(chosen, adjacency, degree, *rows_in, *after)
 
-    def merge(first, mine, theirs, dtypes, *after):
+    def merge(first, skip, mine, theirs, dtypes, *after):
         return pl.pallas_call(
-            functools.partial(merge_kernel, first, len(dtypes)),
+            functools.partial(merge_kernel, first, skip, len(dtypes)),
             out_shape=[jax.ShapeDtypeStruct((tile + EXTRA, width), dtype) for dtype in dtypes],
             in_specs=[VMEM] * (2 + len(after)),
             out_specs=[VMEM] * len(dtypes),
@@ -212,9 +212,11 @@
     first = aggregate(0, far)
     mine = aggregate(1, far + near, first)
     second = aggregate(0, near, mine)
-    parts = merge(0, mine, over_cores(first), [jnp.bfloat16] * len(far))
+    swapped, parts = over_cores(first), []
+    for index in range(len(far)):
+        parts += merge(index, index, mine, swapped, [jnp.bfloat16], *parts[-1:])
     *rest, own = merge(
-        len(far), mine, over_cores(second), [jnp.bfloat16] * (len(near) - 1) + [jnp.float32]
+        len(far), 0, mine, over_cores(second), [jnp.bfloat16] * (len(near) - 1) + [jnp.float32]
     )
     parts = [over_chips(part, step) for step, part in enumerate([*parts, *rest], 1)]
     *parts, last = parts

time: 20.8 us -> 20.8 us (level)
  no operation moved by 1% of the time
where the time goes in v9:
time: 20.8 us; the launch traced here: 20.7 us
  starting transfers between devices  12.7 us (61%)
  Pallas kernels  4.5 us (22%)
  waiting for transfers between devices  3.41 us (16%)
    ppermute x3, starting transfers between devices, over_chips(): return lax.ppermute(array, 'feat', pairs)  6.13 us
    ppermute x3, starting transfers between devices, over_nodes(): return lax.ppermute(feats, 'node', pairs)  5.92 us
    ppermute x3, waiting for transfers between devices, over_chips(): return lax.ppermute(array, 'feat', pairs)  3.31 us
    pallas_call x1, Pallas kernels, body(): pl.pallas_call(prepare_kernel, out_shape=[jax.ShapeDtypeStruct((groups, t...  2.54 us
    pallas_call x3, Pallas kernels, aggregate(): pl.pallas_call(functools.partial(aggregate_kernel, nodes, chips, slots, m...  0.98 us
    pallas_call x1, Pallas kernels, body(): pl.pallas_call(update_kernel, out_shape=jax.ShapeDtypeStruct((tile, width...  0.87 us
    ppermute x2, starting transfers between devices, over_cores(): return lax.ppermute(array, 'feat', [(f, f ^ 1) for f in range(2 * chips)])  0.63 us
  transfers between devices with their start and end apart: 8, of which 3 were waited for; matrix products, arithmetic and copies ran while one was open for 0% of the time, Pallas kernels for 16%

profile of v9, /device:TPU:0, one launch (start us, length us, event | category | flops | bytes accessed | tf_op | source)
XLA Modules:
  0.0 20.7 jit_solution(4430757963987902183)
XLA Ops:
  0.0 2.9 %collective-permute-start = (bf16[128,256]{1,0:T(8,128)(2,1)}, bf16[128,256]{1,0:T(8,128)(2,1)S(1)}, u32[]{:S(2)}, u32[]{:S(2)}) collective-permute-start(bf16[128,256]{1,0:T(8,128)(2,1)} %feats_in.1), channel_id=1, source_target_pairs={{0,8},{8,24},{16,0},{24,16},{1,9},{9,25},{17,1},{25,17},{2,10},{10... | collective-permute-start | bytes 196616 | tf_op jit(solution)/shard_map/ppermute | solution.py:150
  2.9 0.0 collective-permute-start.2
  3.0 3.0 %collective-permute-start.1 = (bf16[128,256]{1,0:T(8,128)(2,1)}, bf16[128,256]{1,0:T(8,128)(2,1)S(1)}, u32[]{:S(2)}, u32[]{:S(2)}) collective-permute-start(bf16[128,256]{1,0:T(8,128)(2,1)} %feats_in.1), channel_id=1, source_target_pairs={{0,24},{8,16},{16,8},{24,0},{1,25},{9,17},{17,9},{25,1},{2,26},{10... | collective-permute-start | bytes 196616 | tf_op jit(solution)/shard_map/ppermute | solution.py:150
  5.9 2.5 %shard_map.64 = (bf16[8,128,384]{2,1,0:T(8,128)(2,1)S(1)}, f32[8,8,128]{2,1,0:T(8,128)S(1)}, s32[24,128]{1,0:T(8,128)S(1)}, bf16[128,256]{1,0:T(8,128)(2,1)S(1)}...) custom-call(s32[1,8]{1,0:T(1,128)} %bitcast.5, s32[3,8]{1,0:T(4,128)} %bitcast.3, bf16[8,3,128,128]{3,2,1,0:T(8,128)(2,1)} %tiles_in.1, ...), custom_call_target="tpu_custom_call" | custom-call | flops 134217728 | bytes 4194304 | tf_op jit(solution)/shard_map/pallas_call | solution.py:160
  8.5 0.0 collective-permute-done.refs_4_
  8.5 0.0 collective-permute-done.2.refs_6_
  8.5 0.0 collective-permute-done.1.refs_5_
  8.5 0.3 %shard_map.65.refs_7_ = bf16[2,136,256]{2,1,0:T(8,128)(2,1)S(1)} custom-call(s32[24,128]{1,0:T(8,128)S(1)} %get-tuple-element.13.refs_0_, bf16[8,128,384]{2,1,0:T(8,128)(2,1)S(1)} %get-tuple-element.14.refs_1_, f32[8,8,128]{2,1,0:T(8,128)S(1)} %get-tuple-element.15.refs_2_, bf16[128,256]{1,0:T(8,128)(2,1)S(1)} %get-tuple-element.16.refs_3_.refs_2_.feats, ...), custom_call_target="tpu_custom_call" | custom-call | flops 134217728 | bytes 4194304 | tf_op jit(solution)/shard_map/pallas_call | solution.py:191
  8.8 0.1 collective-permute-start.4
  8.9 0.4 %shard_map.66.refs_7_.mine = f32[4,136,256]{2,1,0:T(8,128)S(1)} custom-call(s32[24,128]{1,0:T(8,128)S(1)} %get-tuple-element.13.refs_0_, bf16[8,128,384]{2,1,0:T(8,128)(2,1)S(1)} %get-tuple-element.14.refs_1_, f32[8,8,128]{2,1,0:T(8,128)S(1)} %get-tuple-element.15.refs_2_, bf16[128,256]{1,0:T(8,128)(2,1)S(1)} %get-tuple-element.16.refs_3_.refs_2_.feats, ...), custom_call_target="tpu_custom_call" | custom-call | flops 134217728 | bytes 4194304 | tf_op jit(solution)/shard_map/pallas_call | solution.py:191
  9.3 0.3 %shard_map.67 = bf16[2,136,256]{2,1,0:T(8,128)(2,1)S(1)} custom-call(s32[24,128]{1,0:T(8,128)S(1)} %get-tuple-element.13.refs_0_, bf16[8,128,384]{2,1,0:T(8,128)(2,1)S(1)} %get-tuple-element.14.refs_1_, f32[8,8,128]{2,1,0:T(8,128)S(1)} %get-tuple-element.15.refs_2_, bf16[128,256]{1,0:T(8,128)(2,1)S(1)} %get-tuple-element.16.refs_3_.refs_2_.feats, ...), custom_call_target="tpu_custom_call" | custom-call | flops 134217728 | bytes 4194304 | tf_op jit(solution)/shard_map/pallas_call | solution.py:191
  9.6 0.6 %collective-permute-start.3 = (bf16[2,136,256]{2,1,0:T(8,128)(2,1)S(1)}, bf16[2,136,256]{2,1,0:T(8,128)(2,1)S(1)}, u32[]{:S(2)}, u32[]{:S(2)}) collective-permute-start(bf16[2,136,256]{2,1,0:T(8,128)(2,1)S(1)} %shard_map.67), channel_id=1, source_target_pairs={{0,1},{1,0},{2,3},{3,2},{4,5},{5,4},{6,7},{7,6},{8,9},{9,8},{10,11... | collective-permute-start | bytes 417800 | tf_op jit(solution)/shard_map/ppermute | solution.py:157
  10.1 0.1 collective-permute-done.4.theirs
  10.3 2.0 %collective-permute-start.5 = (bf16[136,256]{1,0:T(8,128)(2,1)S(1)}, bf16[136,256]{1,0:T(8,128)(2,1)S(1)}, u32[]{:S(2)}, u32[]{:S(2)}) collective-permute-start(bf16[136,256]{1,0:T(8,128)(2,1)S(1)} %shard_map.69.outs_0_), channel_id=1, source_target_pairs={{0,2},{1,3},{2,6},{3,7},{4,0},{5,1},{6,4},{7,5},{8,10},{9,11},{10,... | collective-permute-start | bytes 208904 | tf_op jit(solution)/shard_map/ppermute | solution.py:154
  12.3 2.5 %collective-permute-start.6 = (bf16[136,256]{1,0:T(8,128)(2,1)S(1)}, bf16[136,256]{1,0:T(8,128)(2,1)S(1)}, u32[]{:S(2)}, u32[]{:S(2)}) collective-permute-start(bf16[136,256]{1,0:T(8,128)(2,1)S(1)} %shard_map.70), channel_id=1, source_target_pairs={{0,6},{1,7},{2,4},{3,5},{4,2},{5,3},{6,0},{7,1},{8,14},{9,15},{10,... | collective-permute-start | bytes 208904 | tf_op jit(solution)/shard_map/ppermute | solution.py:154
  14.8 0.0 collective-permute-done.3.theirs
  14.8 1.6 %collective-permute-start.7 = (bf16[136,256]{1,0:T(8,128)(2,1)S(1)}, bf16[136,256]{1,0:T(8,128)(2,1)S(1)}, u32[]{:S(2)}, u32[]{:S(2)}) collective-permute-start(bf16[136,256]{1,0:T(8,128)(2,1)S(1)} %get-tuple-element.18), channel_id=1, source_target_pairs={{0,4},{1,5},{2,0},{3,1},{4,6},{5,7},{6,2},{7,3},{8,12},{9,13},{10,... | collective-permute-start | bytes 208904 | tf_op jit(solution)/shard_map/ppermute | solution.py:154
  16.5 2.8 %collective-permute-done.6.refs_1_ = bf16[136,256]{1,0:T(8,128)(2,1)S(1)} collective-permute-done((bf16[136,256]{1,0:T(8,128)(2,1)S(1)}, bf16[136,256]{1,0:T(8,128)(2,1)S(1)}, u32[]{:S(2)}, u32[]{:S(2)}) %collective-permute-start.6) | collective-permute-done | bytes 69664 | tf_op jit(solution)/shard_map/ppermute | solution.py:154
  19.2 0.0 collective-permute-done.5.refs_0_
  19.3 0.5 %collective-permute-done.7.last = bf16[136,256]{1,0:T(8,128)(2,1)S(1)} collective-permute-done((bf16[136,256]{1,0:T(8,128)(2,1)S(1)}, bf16[136,256]{1,0:T(8,128)(2,1)S(1)}, u32[]{:S(2)}, u32[]{:S(2)}) %collective-permute-start.7) | collective-permute-done | bytes 69664 | tf_op jit(solution)/shard_map/ppermute | solution.py:154
  19.8 0.9 %shard_map.72 = bf16[128,256]{1,0:T(8,128)(2,1)} custom-call(f32[136,256]{1,0:T(8,128)S(1)} %shard_map.71.earlier, bf16[136,256]{1,0:T(8,128)(2,1)S(1)} %collective-permute-done.7.last, bf16[128,256]{1,0:T(8,128)(2,1)S(1)} %get-tuple-element.16.refs_3_.refs_2_.feats, bf16[256,256]{1,0:T(8,128)(2,1)S(1)} %get-tuple-element.19.weight, ...), custom_call_target="tpu_custom_call" | custom-call | tf_op jit(solution)/shard_map/pallas_call | solution.py:230
  (4 shorter events, 0.1 us)
Async XLA Ops:
  0.0 8.5 %collective-permute-start = (bf16[128,256]{1,0:T(8,128)(2,1)}, bf16[128,256]{1,0:T(8,128)(2,1)S(1)}, u32[]{:S(2)}, u32[]{:S(2)}) collective-permute-start(bf16[128,256]{1,0:T(8,128)(2,1)} %feats_in.1), channel_id=1, source_target_pairs={{0,8},{8,24},{16,0},{24,16},{1,9},{9,25},{17,1},{25,17},{2,10},{10... | collective-permute-start | bytes 196616 | tf_op jit(solution)/shard_map/ppermute | solution.py:150
  2.9 5.5 %collective-permute-start.2 = (bf16[128,256]{1,0:T(8,128)(2,1)}, bf16[128,256]{1,0:T(8,128)(2,1)S(1)}, u32[]{:S(2)}, u32[]{:S(2)}) collective-permute-start(bf16[128,256]{1,0:T(8,128)(2,1)} %feats_in.1), channel_id=1, source_target_pairs={{0,16},{8,0},{16,24},{24,8},{1,17},{9,1},{17,25},{25,9},{2,18},{10... | collective-permute-start | bytes 196616 | tf_op jit(solution)/shard_map/ppermute | solution.py:150
  3.0 5.5 %collective-permute-start.1 = (bf16[128,256]{1,0:T(8,128)(2,1)}, bf16[128,256]{1,0:T(8,128)(2,1)S(1)}, u32[]{:S(2)}, u32[]{:S(2)}) collective-permute-start(bf16[128,256]{1,0:T(8,128)(2,1)} %feats_in.1), channel_id=1, source_target_pairs={{0,24},{8,16},{16,8},{24,0},{1,25},{9,17},{17,9},{25,1},{2,26},{10... | collective-permute-start | bytes 196616 | tf_op jit(solution)/shard_map/ppermute | solution.py:150
  8.8 1.4 %collective-permute-start.4 = (bf16[2,136,256]{2,1,0:T(8,128)(2,1)S(1)}, bf16[2,136,256]{2,1,0:T(8,128)(2,1)S(1)}, u32[]{:S(2)}, u32[]{:S(2)}) collective-permute-start(bf16[2,136,256]{2,1,0:T(8,128)(2,1)S(1)} %shard_map.65.refs_7_), channel_id=1, source_target_pairs={{0,1},{1,0},{2,3},{3,2},{4,5},{5,4},{6,7},{7,6},{8,9},{9,8},{10,11... | collective-permute-start | bytes 417800 | tf_op jit(solution)/shard_map/ppermute | solution.py:157
  9.6 5.2 %collective-permute-start.3 = (bf16[2,136,256]{2,1,0:T(8,128)(2,1)S(1)}, bf16[2,136,256]{2,1,0:T(8,128)(2,1)S(1)}, u32[]{:S(2)}, u32[]{:S(2)}) collective-permute-start(bf16[2,136,256]{2,1,0:T(8,128)(2,1)S(1)} %shard_map.67), channel_id=1, source_target_pairs={{0,1},{1,0},{2,3},{3,2},{4,5},{5,4},{6,7},{7,6},{8,9},{9,8},{10,11... | collective-permute-start | bytes 417800 | tf_op jit(solution)/shard_map/ppermute | solution.py:157
  10.3 9.0 %collective-permute-start.5 = (bf16[136,256]{1,0:T(8,128)(2,1)S(1)}, bf16[136,256]{1,0:T(8,128)(2,1)S(1)}, u32[]{:S(2)}, u32[]{:S(2)}) collective-permute-start(bf16[136,256]{1,0:T(8,128)(2,1)S(1)} %shard_map.69.outs_0_), channel_id=1, source_target_pairs={{0,2},{1,3},{2,6},{3,7},{4,0},{5,1},{6,4},{7,5},{8,10},{9,11},{10,... | collective-permute-start | bytes 208904 | tf_op jit(solution)/shard_map/ppermute | solution.py:154
  12.3 7.0 %collective-permute-start.6 = (bf16[136,256]{1,0:T(8,128)(2,1)S(1)}, bf16[136,256]{1,0:T(8,128)(2,1)S(1)}, u32[]{:S(2)}, u32[]{:S(2)}) collective-permute-start(bf16[136,256]{1,0:T(8,128)(2,1)S(1)} %shard_map.70), channel_id=1, source_target_pairs={{0,6},{1,7},{2,4},{3,5},{4,2},{5,3},{6,0},{7,1},{8,14},{9,15},{10,... | collective-permute-start | bytes 208904 | tf_op jit(solution)/shard_map/ppermute | solution.py:154
  14.8 5.0 %collective-permute-start.7 = (bf16[136,256]{1,0:T(8,128)(2,1)S(1)}, bf16[136,256]{1,0:T(8,128)(2,1)S(1)}, u32[]{:S(2)}, u32[]{:S(2)}) collective-permute-start(bf16[136,256]{1,0:T(8,128)(2,1)S(1)} %get-tuple-element.18), channel_id=1, source_target_pairs={{0,4},{1,5},{2,0},{3,1},{4,6},{5,7},{6,2},{7,3},{8,12},{9,13},{10,... | collective-permute-start | bytes 208904 | tf_op jit(solution)/shard_map/ppermute | solution.py:154
